TPU v7x, 128 devices: a whole 4x4x4 slice. The times are simulated.
128 devices in a mesh: row: 8 (over x, core), col: 16 (over z, y).
Axes of the slice: x: 4, y: 4, z: 4, core: 2. Of those that a mesh axis runs over, the one named last changes fastest.
Arguments:
- vertex_panel: bfloat16 [32768, 512], P('row'), may hold values from -1.1953125 to 1.1953125
- context_panel: bfloat16 [8192, 512], P('col'), may hold values from -1.1953125 to 1.1953125
- hot_table: bfloat16 [1024, 512], replicated, may hold values from -1.1953125 to 1.1953125
- matching: int32 [2, 16], replicated, may hold values from 0 to 15, as said below
- hot_map: int32 [8, 16, 256], P('row', 'col'), may hold values from 0 to 1023
- cold_list: int32 [8, 16, 16, 64], P('row'), may hold values from 0 to 255
- cold_count: int32 [8, 16, 16], P('row'), may hold values from 17 to 64, as said below
- src_code: int32 [8, 16, 2, 128, 128], P('row', 'col'), may hold values from 0 to 1279, as said below
- ctx_rows: int32 [8, 16, 2, 128, 128], P('row', 'col'), may hold values from 0 to 511
- neg_tiles: int32 [8, 16, 2, 128], P('row', 'col'), may hold values from 0 to 3
Outputs:
- vertex_new: float32 [32768, 512], P(('row', 'col'))
- context_new: float32 [8192, 512], P('col')
- hot_new: float32 [1024, 512], replicated
Inputs may be any that keep to these rules, and one draw needn't show every extreme that they name: In sub-episode s every partition c is paired with matching[s, c] = c xor m_s, with one number m_s of 1 to 15 common to all c. `cold_count`: in each vertex partition some owner receives exactly 64 live slots from every sender. `src_code`: A code below 256 names hot slot code; a code j + 256 names cold slot k = j % 64 of owner o = j // 64, and then k < cold_count[r, c, o].
All inputs are finite; a program needn't handle non-finite values.
Results may differ from a plain program's by a relative error of at most 0.0033.
Values may be sent and summed in bfloat16 or wider, within the bound.
No kernel may reach another device: no remote copies, remote signals or barrier semaphores. Data moves between devices by JAX's collectives and lax.ppermute only.
A program may use at most 128 MiB of HBM per device.

v0:
```python
import jax
import jax.numpy as jnp
from jax import lax
from jax.sharding import PartitionSpec as P

NEG_WEIGHT = 0.0625
LEARN_RATE = 0.25


def swapped(x, axis, distance):
    return lax.ppermute(x, axis, [(i, i ^ 1 << distance) for i in range(lax.axis_size(axis))])


def episode_grads(slot_table, codes, row_ids, tile_ids, ctx_panel):
    width = slot_table.shape[1]
    block_rows = codes.shape[1]
    group_size = min(16, codes.shape[0])
    tile_view = ctx_panel.reshape(-1, block_rows, width)

    def one_group(totals, inputs):
        slot_grad, context_grad, tile_grad = totals
        code_group, row_group, tile_group = inputs
        sources = slot_table[code_group]
        positive = ctx_panel[row_group]
        negative = tile_view[tile_group]
        pos_score = jnp.einsum("gbd,gbd->gb", sources, positive, preferred_element_type=jnp.float32)
        neg_score = jnp.einsum(
            "gid,gjd->gij", sources, negative, preferred_element_type=jnp.float32
        )
        pos_grad = -jax.nn.sigmoid(-pos_score)
        neg_grad = (NEG_WEIGHT * jax.nn.sigmoid(neg_score)).astype(jnp.bfloat16)
        source_grad = pos_grad[..., None] * positive + jnp.einsum(
            "gij,gjd->gid", neg_grad, negative, preferred_element_type=jnp.float32
        )
        slot_grad = slot_grad.at[code_group.reshape(-1)].add(source_grad.reshape(-1, width))
        context_grad = context_grad.at[row_group.reshape(-1)].add(
            (pos_grad[..., None] * sources).reshape(-1, width)
        )
        tile_grad = tile_grad.at[tile_group].add(
            jnp.einsum("gij,gid->gjd", neg_grad, sources, preferred_element_type=jnp.float32)
        )
        return ((slot_grad, context_grad, tile_grad), None)

    start_totals = (
        jnp.zeros(slot_table.shape, jnp.float32),
        jnp.zeros(ctx_panel.shape, jnp.float32),
        jnp.zeros(tile_view.shape, jnp.float32),
    )
    inputs = (
        codes.reshape(-1, group_size, block_rows),
        row_ids.reshape(-1, group_size, block_rows),
        tile_ids.reshape(-1, group_size),
    )
    totals, unused = lax.scan(one_group, start_totals, inputs)
    return (totals[0], totals[1] + totals[2].reshape(-1, width))


def slot_rows(part_panel, hot_table, hot_list, own_lists, own_counts):
    col_count, capacity = own_lists.shape
    per_owner = part_panel.shape[0] // col_count
    cold_ids = (jnp.arange(col_count, dtype=jnp.int32)[:, None] * per_owner + own_lists).reshape(-1)
    in_list = (jnp.arange(capacity, dtype=jnp.int32)[None, :] < own_counts[:, None]).reshape(-1, 1)
    cold_emb = jnp.where(in_list, part_panel[cold_ids], jnp.zeros((), part_panel.dtype))
    return (jnp.concatenate([hot_table[hot_list], cold_emb], 0), in_list)


def route_panel(moving, xor_mask):
    for bit_number in range(lax.axis_size("col").bit_length() - 1):
        is_set = xor_mask // (1 << bit_number) % 2 == 1
        arrived = swapped(moving, "col", bit_number)
        moving = jnp.where(is_set, arrived, moving)
    return moving


def route_grads(moving, xor_mask):
    for bit_number in range(lax.axis_size("col").bit_length() - 1):
        is_set = xor_mask // (1 << bit_number) % 2 == 1
        arrived = swapped(moving, "col", bit_number)
        moving = jnp.where(is_set, arrived, moving)
    return moving


def body(
    vertex_panel,
    context_panel,
    hot_table,
    matching,
    hot_map,
    cold_list,
    cold_count,
    src_code,
    ctx_rows,
    neg_tiles,
):
    col_index = lax.axis_index("col")
    col_count = lax.axis_size("col")
    width = vertex_panel.shape[1]
    owned_rows = vertex_panel.shape[0] // col_count
    capacity = cold_list.shape[-1]
    hot_list = hot_map[0, 0]
    hot_slots = hot_list.shape[0]
    slot_table, in_list = slot_rows(
        vertex_panel, hot_table, hot_list, cold_list[0][col_index], cold_count[0][col_index]
    )
    slot_total = jnp.zeros(slot_table.shape, jnp.float32)
    hot_summed = jnp.zeros(hot_table.shape, jnp.float32)
    context_total = jnp.zeros(context_panel.shape, jnp.float32)
    for episode in range(src_code.shape[2]):
        xor_mask = jnp.bitwise_xor(matching[episode, 0], jnp.int32(0))
        ctx_panel = route_panel(context_panel, xor_mask)
        slot_grad, context_grad = episode_grads(
            slot_table,
            src_code[0, 0, episode],
            ctx_rows[0, 0, episode],
            neg_tiles[0, 0, episode],
            ctx_panel,
        )
        slot_total = slot_total + slot_grad
        hot_local = jnp.zeros(hot_table.shape, jnp.float32).at[hot_list].add(slot_grad[:hot_slots])
        hot_summed = hot_summed + lax.psum(hot_local, ("row", "col"))
        summed = lax.psum(context_grad, "row").astype(jnp.bfloat16)
        returned = route_grads(summed, xor_mask)
        context_total = context_total + returned.astype(jnp.float32)
    hot_new = hot_table.astype(jnp.float32) - LEARN_RATE * hot_summed
    cold_grad = jnp.where(in_list, slot_total[hot_slots:], 0.0).reshape(col_count, capacity, width)
    received = lax.all_to_all(cold_grad, "col", split_axis=0, concat_axis=0, tiled=True)
    sender_lists = cold_list[0][:, col_index]
    vertex_grad = (
        jnp.zeros((owned_rows, width), jnp.float32)
        .at[sender_lists.reshape(-1)]
        .add(received.reshape(-1, width))
    )
    owned = lax.dynamic_slice_in_dim(vertex_panel, col_index * owned_rows, owned_rows, 0)
    vertex_new = owned.astype(jnp.float32) - LEARN_RATE * vertex_grad
    context_new = context_panel.astype(jnp.float32) - LEARN_RATE * context_total
    return (vertex_new, context_new, hot_new)


def solution(mesh):
    in_specs = (
        P("row", None),
        P("col", None),
        P(),
        P(),
        P("row", "col", None),
        P("row", None, None, None),
        P("row", None, None),
        P("row", "col", None, None, None),
        P("row", "col", None, None, None),
        P("row", "col", None, None),
    )
    out_specs = (P(("row", "col"), None), P("col", None), P())
    return jax.shard_map(body, mesh=mesh, in_specs=in_specs, out_specs=out_specs, check_vma=False)
```

profile of v0, /device:TPU:1, one launch (start us, length us, event | category | flops | bytes accessed | tf_op | source)
XLA Modules:
  0.0 1571.5 jit_solution(10859683056158333559)
XLA Ops:
  84.5 596.1 %while.29 = (s32[]{:T(128)}, f32[1280,512]{1,0:T(8,128)}, f32[512,512]{1,0:T(8,128)}, f32[4,128,512]{2,1,0:T(8,128)S(1)}, s32[8,16,128]{2,1,0:T(8,128)}, /*index...) while((s32[]{:T(128)}, f32[1280,512]{1,0:T(8,128)}, ...), condition=%wide.region_9.10_spmd, body=%wide.region_5.9_spmd.sunk | while | flops 819233856 | bytes 90862664 | solution.py:54
  115.2 16.5 %scatter_fusion.2 = f32[1280,512]{1,0:T(8,128)} fusion(f32[1280,512]{1,0:T(8,128)} %get-tuple-element.345, s32[2048]{0:T(1024)S(1)} %bitcast.190, f32[2048,512]{1,0:T(8,128)} %bitcast.187), kind=kCustom, calls=%fused_computation.11.clone.1 | custom fusion | flops 1048576 | bytes 12591104 | tf_op jit(solution)/shard_map/while/body/eval_jaxpr/scatter-add | solution.py:35
  189.7 16.5 %scatter_fusion.2 = f32[1280,512]{1,0:T(8,128)} fusion(f32[1280,512]{1,0:T(8,128)} %get-tuple-element.345, s32[2048]{0:T(1024)S(1)} %bitcast.190, f32[2048,512]{1,0:T(8,128)} %bitcast.187), kind=kCustom, calls=%fused_computation.11.clone.1 | custom fusion | flops 1048576 | bytes 12591104 | tf_op jit(solution)/shard_map/while/body/eval_jaxpr/scatter-add | solution.py:35
  206.9 16.3 %scatter_custom_fusion.28 = f32[512,512]{1,0:T(8,128)} fusion(f32[512,512]{1,0:T(8,128)} %get-tuple-element.346, s32[2048]{0:T(1024)S(1)} %bitcast.196, bf16[2048,512]{1,0:T(8,128)(2,1)} %gather_fusion.4, f32[2048]{0:T(1024)S(1)} %get-tuple-element.332), kind=kCustom, calls=%fused_computation.52.clone.1 | custom fusion | flops 3145728 | bytes 3153920 | tf_op jit(solution)/shard_map/while/body/eval_jaxpr/scatter-add | solution.py:36
  264.2 16.5 %scatter_fusion.2 = f32[1280,512]{1,0:T(8,128)} fusion(f32[1280,512]{1,0:T(8,128)} %get-tuple-element.345, s32[2048]{0:T(1024)S(1)} %bitcast.190, f32[2048,512]{1,0:T(8,128)} %bitcast.187), kind=kCustom, calls=%fused_computation.11.clone.1 | custom fusion | flops 1048576 | bytes 12591104 | tf_op jit(solution)/shard_map/while/body/eval_jaxpr/scatter-add | solution.py:35
  281.4 16.3 %scatter_custom_fusion.28 = f32[512,512]{1,0:T(8,128)} fusion(f32[512,512]{1,0:T(8,128)} %get-tuple-element.346, s32[2048]{0:T(1024)S(1)} %bitcast.196, bf16[2048,512]{1,0:T(8,128)(2,1)} %gather_fusion.4, f32[2048]{0:T(1024)S(1)} %get-tuple-element.332), kind=kCustom, calls=%fused_computation.52.clone.1 | custom fusion | flops 3145728 | bytes 3153920 | tf_op jit(solution)/shard_map/while/body/eval_jaxpr/scatter-add | solution.py:36
  338.7 16.5 %scatter_fusion.2 = f32[1280,512]{1,0:T(8,128)} fusion(f32[1280,512]{1,0:T(8,128)} %get-tuple-element.345, s32[2048]{0:T(1024)S(1)} %bitcast.190, f32[2048,512]{1,0:T(8,128)} %bitcast.187), kind=kCustom, calls=%fused_computation.11.clone.1 | custom fusion | flops 1048576 | bytes 12591104 | tf_op jit(solution)/shard_map/while/body/eval_jaxpr/scatter-add | solution.py:35
  413.3 16.5 %scatter_fusion.2 = f32[1280,512]{1,0:T(8,128)} fusion(f32[1280,512]{1,0:T(8,128)} %get-tuple-element.345, s32[2048]{0:T(1024)S(1)} %bitcast.190, f32[2048,512]{1,0:T(8,128)} %bitcast.187), kind=kCustom, calls=%fused_computation.11.clone.1 | custom fusion | flops 1048576 | bytes 12591104 | tf_op jit(solution)/shard_map/while/body/eval_jaxpr/scatter-add | solution.py:35
  430.4 16.3 %scatter_custom_fusion.28 = f32[512,512]{1,0:T(8,128)} fusion(f32[512,512]{1,0:T(8,128)} %get-tuple-element.346, s32[2048]{0:T(1024)S(1)} %bitcast.196, bf16[2048,512]{1,0:T(8,128)(2,1)} %gather_fusion.4, f32[2048]{0:T(1024)S(1)} %get-tuple-element.332), kind=kCustom, calls=%fused_computation.52.clone.1 | custom fusion | flops 3145728 | bytes 3153920 | tf_op jit(solution)/shard_map/while/body/eval_jaxpr/scatter-add | solution.py:36
  487.8 16.5 %scatter_fusion.2 = f32[1280,512]{1,0:T(8,128)} fusion(f32[1280,512]{1,0:T(8,128)} %get-tuple-element.345, s32[2048]{0:T(1024)S(1)} %bitcast.190, f32[2048,512]{1,0:T(8,128)} %bitcast.187), kind=kCustom, calls=%fused_computation.11.clone.1 | custom fusion | flops 1048576 | bytes 12591104 | tf_op jit(solution)/shard_map/while/body/eval_jaxpr/scatter-add | solution.py:35
  562.3 16.5 %scatter_fusion.2 = f32[1280,512]{1,0:T(8,128)} fusion(f32[1280,512]{1,0:T(8,128)} %get-tuple-element.345, s32[2048]{0:T(1024)S(1)} %bitcast.190, f32[2048,512]{1,0:T(8,128)} %bitcast.187), kind=kCustom, calls=%fused_computation.11.clone.1 | custom fusion | flops 1048576 | bytes 12591104 | tf_op jit(solution)/shard_map/while/body/eval_jaxpr/scatter-add | solution.py:35
  636.8 16.5 %scatter_fusion.2 = f32[1280,512]{1,0:T(8,128)} fusion(f32[1280,512]{1,0:T(8,128)} %get-tuple-element.345, s32[2048]{0:T(1024)S(1)} %bitcast.190, f32[2048,512]{1,0:T(8,128)} %bitcast.187), kind=kCustom, calls=%fused_computation.11.clone.1 | custom fusion | flops 1048576 | bytes 12591104 | tf_op jit(solution)/shard_map/while/body/eval_jaxpr/scatter-add | solution.py:35
  685.3 597.0 %while.28 = (s32[]{:T(128)}, f32[1280,512]{1,0:T(8,128)}, f32[512,512]{1,0:T(8,128)}, f32[4,128,512]{2,1,0:T(8,128)S(1)}, s32[8,16,128]{2,1,0:T(8,128)}, /*index...) while((s32[]{:T(128)}, f32[1280,512]{1,0:T(8,128)}, ...), condition=%wide.region_4.5_spmd, body=%wide.region_0.4_spmd.sunk | while | flops 819233856 | bytes 90862664 | solution.py:54
  716.2 16.5 %scatter_fusion = f32[1280,512]{1,0:T(8,128)} fusion(f32[1280,512]{1,0:T(8,128)} %get-tuple-element.378, s32[2048]{0:T(1024)S(1)} %bitcast.191, f32[2048,512]{1,0:T(8,128)} %bitcast.188), kind=kCustom, calls=%fused_computation.8.clone.1 | custom fusion | flops 1048576 | bytes 12591104 | tf_op jit(solution)/shard_map/while/body/eval_jaxpr/scatter-add | solution.py:35
  733.4 16.3 %scatter_custom_fusion.24 = f32[512,512]{1,0:T(8,128)} fusion(f32[512,512]{1,0:T(8,128)} %get-tuple-element.379, s32[2048]{0:T(1024)S(1)} %bitcast.197, bf16[2048,512]{1,0:T(8,128)(2,1)} %gather_fusion.1, f32[2048]{0:T(1024)S(1)} %get-tuple-element.316), kind=kCustom, calls=%fused_computation.22.clone.1 | custom fusion | flops 3145728 | bytes 3153920 | tf_op jit(solution)/shard_map/while/body/eval_jaxpr/scatter-add | solution.py:36
  790.8 16.5 %scatter_fusion = f32[1280,512]{1,0:T(8,128)} fusion(f32[1280,512]{1,0:T(8,128)} %get-tuple-element.378, s32[2048]{0:T(1024)S(1)} %bitcast.191, f32[2048,512]{1,0:T(8,128)} %bitcast.188), kind=kCustom, calls=%fused_computation.8.clone.1 | custom fusion | flops 1048576 | bytes 12591104 | tf_op jit(solution)/shard_map/while/body/eval_jaxpr/scatter-add | solution.py:35
  808.0 16.3 %scatter_custom_fusion.24 = f32[512,512]{1,0:T(8,128)} fusion(f32[512,512]{1,0:T(8,128)} %get-tuple-element.379, s32[2048]{0:T(1024)S(1)} %bitcast.197, bf16[2048,512]{1,0:T(8,128)(2,1)} %gather_fusion.1, f32[2048]{0:T(1024)S(1)} %get-tuple-element.316), kind=kCustom, calls=%fused_computation.22.clone.1 | custom fusion | flops 3145728 | bytes 3153920 | tf_op jit(solution)/shard_map/while/body/eval_jaxpr/scatter-add | solution.py:36
  865.4 16.5 %scatter_fusion = f32[1280,512]{1,0:T(8,128)} fusion(f32[1280,512]{1,0:T(8,128)} %get-tuple-element.378, s32[2048]{0:T(1024)S(1)} %bitcast.191, f32[2048,512]{1,0:T(8,128)} %bitcast.188), kind=kCustom, calls=%fused_computation.8.clone.1 | custom fusion | flops 1048576 | bytes 12591104 | tf_op jit(solution)/shard_map/while/body/eval_jaxpr/scatter-add | solution.py:35
  882.6 16.3 %scatter_custom_fusion.24 = f32[512,512]{1,0:T(8,128)} fusion(f32[512,512]{1,0:T(8,128)} %get-tuple-element.379, s32[2048]{0:T(1024)S(1)} %bitcast.197, bf16[2048,512]{1,0:T(8,128)(2,1)} %gather_fusion.1, f32[2048]{0:T(1024)S(1)} %get-tuple-element.316), kind=kCustom, calls=%fused_computation.22.clone.1 | custom fusion | flops 3145728 | bytes 3153920 | tf_op jit(solution)/shard_map/while/body/eval_jaxpr/scatter-add | solution.py:36
  940.0 16.5 %scatter_fusion = f32[1280,512]{1,0:T(8,128)} fusion(f32[1280,512]{1,0:T(8,128)} %get-tuple-element.378, s32[2048]{0:T(1024)S(1)} %bitcast.191, f32[2048,512]{1,0:T(8,128)} %bitcast.188), kind=kCustom, calls=%fused_computation.8.clone.1 | custom fusion | flops 1048576 | bytes 12591104 | tf_op jit(solution)/shard_map/while/body/eval_jaxpr/scatter-add | solution.py:35
  957.2 16.3 %scatter_custom_fusion.24 = f32[512,512]{1,0:T(8,128)} fusion(f32[512,512]{1,0:T(8,128)} %get-tuple-element.379, s32[2048]{0:T(1024)S(1)} %bitcast.197, bf16[2048,512]{1,0:T(8,128)(2,1)} %gather_fusion.1, f32[2048]{0:T(1024)S(1)} %get-tuple-element.316), kind=kCustom, calls=%fused_computation.22.clone.1 | custom fusion | flops 3145728 | bytes 3153920 | tf_op jit(solution)/shard_map/while/body/eval_jaxpr/scatter-add | solution.py:36
  1014.6 16.5 %scatter_fusion = f32[1280,512]{1,0:T(8,128)} fusion(f32[1280,512]{1,0:T(8,128)} %get-tuple-element.378, s32[2048]{0:T(1024)S(1)} %bitcast.191, f32[2048,512]{1,0:T(8,128)} %bitcast.188), kind=kCustom, calls=%fused_computation.8.clone.1 | custom fusion | flops 1048576 | bytes 12591104 | tf_op jit(solution)/shard_map/while/body/eval_jaxpr/scatter-add | solution.py:35
  1031.8 16.3 %scatter_custom_fusion.24 = f32[512,512]{1,0:T(8,128)} fusion(f32[512,512]{1,0:T(8,128)} %get-tuple-element.379, s32[2048]{0:T(1024)S(1)} %bitcast.197, bf16[2048,512]{1,0:T(8,128)(2,1)} %gather_fusion.1, f32[2048]{0:T(1024)S(1)} %get-tuple-element.316), kind=kCustom, calls=%fused_computation.22.clone.1 | custom fusion | flops 3145728 | bytes 3153920 | tf_op jit(solution)/shard_map/while/body/eval_jaxpr/scatter-add | solution.py:36
  1089.2 16.5 %scatter_fusion = f32[1280,512]{1,0:T(8,128)} fusion(f32[1280,512]{1,0:T(8,128)} %get-tuple-element.378, s32[2048]{0:T(1024)S(1)} %bitcast.191, f32[2048,512]{1,0:T(8,128)} %bitcast.188), kind=kCustom, calls=%fused_computation.8.clone.1 | custom fusion | flops 1048576 | bytes 12591104 | tf_op jit(solution)/shard_map/while/body/eval_jaxpr/scatter-add | solution.py:35
  1106.4 16.3 %scatter_custom_fusion.24 = f32[512,512]{1,0:T(8,128)} fusion(f32[512,512]{1,0:T(8,128)} %get-tuple-element.379, s32[2048]{0:T(1024)S(1)} %bitcast.197, bf16[2048,512]{1,0:T(8,128)(2,1)} %gather_fusion.1, f32[2048]{0:T(1024)S(1)} %get-tuple-element.316), kind=kCustom, calls=%fused_computation.22.clone.1 | custom fusion | flops 3145728 | bytes 3153920 | tf_op jit(solution)/shard_map/while/body/eval_jaxpr/scatter-add | solution.py:36
  1163.8 16.5 %scatter_fusion = f32[1280,512]{1,0:T(8,128)} fusion(f32[1280,512]{1,0:T(8,128)} %get-tuple-element.378, s32[2048]{0:T(1024)S(1)} %bitcast.191, f32[2048,512]{1,0:T(8,128)} %bitcast.188), kind=kCustom, calls=%fused_computation.8.clone.1 | custom fusion | flops 1048576 | bytes 12591104 | tf_op jit(solution)/shard_map/while/body/eval_jaxpr/scatter-add | solution.py:35
  1181.0 16.3 %scatter_custom_fusion.24 = f32[512,512]{1,0:T(8,128)} fusion(f32[512,512]{1,0:T(8,128)} %get-tuple-element.379, s32[2048]{0:T(1024)S(1)} %bitcast.197, bf16[2048,512]{1,0:T(8,128)(2,1)} %gather_fusion.1, f32[2048]{0:T(1024)S(1)} %get-tuple-element.316), kind=kCustom, calls=%fused_computation.22.clone.1 | custom fusion | flops 3145728 | bytes 3153920 | tf_op jit(solution)/shard_map/while/body/eval_jaxpr/scatter-add | solution.py:36
  1238.4 16.5 %scatter_fusion = f32[1280,512]{1,0:T(8,128)} fusion(f32[1280,512]{1,0:T(8,128)} %get-tuple-element.378, s32[2048]{0:T(1024)S(1)} %bitcast.191, f32[2048,512]{1,0:T(8,128)} %bitcast.188), kind=kCustom, calls=%fused_computation.8.clone.1 | custom fusion | flops 1048576 | bytes 12591104 | tf_op jit(solution)/shard_map/while/body/eval_jaxpr/scatter-add | solution.py:35
  1255.6 16.3 %scatter_custom_fusion.24 = f32[512,512]{1,0:T(8,128)} fusion(f32[512,512]{1,0:T(8,128)} %get-tuple-element.379, s32[2048]{0:T(1024)S(1)} %bitcast.197, bf16[2048,512]{1,0:T(8,128)(2,1)} %gather_fusion.1, f32[2048]{0:T(1024)S(1)} %get-tuple-element.316), kind=kCustom, calls=%fused_computation.22.clone.1 | custom fusion | flops 3145728 | bytes 3153920 | tf_op jit(solution)/shard_map/while/body/eval_jaxpr/scatter-add | solution.py:36
  1287.4 55.0 %all-reduce.5 = (bf16[512,512]{1,0:T(8,128)(2,1)S(1)}, bf16[512,512]{1,0:T(8,128)(2,1)}) all-reduce(f32[512,512]{1,0:T(8,128)} %get-tuple-element.185, f32[512,512]{1,0:T(8,128)} %get-tuple-element.186), channel_id=1, replica_groups=mesh['row'=8,'col'=16] {'row'}, use_global_device_ids=true, to_apply=%region_12.13 | all-reduce | flops 524288 | bytes 3145728 | tf_op jit(solution)/shard_map/psum | solution.py:121
  1383.6 33.1 %collective-permute-done.8 = bf16[512,512]{1,0:T(8,128)(2,1)} collective-permute-done((bf16[512,512]{1,0:T(8,128)(2,1)}, bf16[512,512]{1,0:T(8,128)(2,1)}, u32[]{:S(2)}, u32[]{:S(2)}) %collective-permute-start.8) | collective-permute-done | bytes 524320 | tf_op jit(solution)/shard_map/ppermute | solution.py:11
  1430.7 119.7 %all-reduce.4.cloned.1.call-done = f32[1024,512]{1,0:T(8,128)} async-done(((f32[1024,512]{1,0:T(8,128)}), f32[1024,512]{1,0:T(8,128)}) %all-reduce.4.cloned.1.call-update) | async-done | bytes 2097168 | tf_op jit(solution)/shard_map/psum | solution.py:120
  (499 shorter events, 899.8 us)
Async XLA Ops:
  7.2 9.0 copy-start
  7.2 18.8 %collective-permute-start = (bf16[512,512]{1,0:T(8,128)(2,1)}, bf16[512,512]{1,0:T(8,128)(2,1)}, u32[]{:S(2)}, u32[]{:S(2)}) collective-permute-start(bf16[512,512]{1,0:T(8,128)(2,1)} %param.15), channel_id=1, source_target_pairs={{0,1},{1,0},{2,3},{3,2},{4,5},{5,4},{6,7},{7,6},{8,9},{9,8},{10,11... | collective-permute-start | bytes 1572872 | tf_op jit(solution)/shard_map/ppermute | solution.py:11
  17.1 27.3 %copy-start.18 = (pred[1024]{0:T(1024)(128)(4,1)}, pred[1024]{0:T(1024)(128)(4,1)S(1)}, u32[]{:S(2)}) copy-start(pred[1024]{0:T(1024)(128)(4,1)S(1)} %lt.227) | copy-start | bytes 3076
  19.2 6.7 copy-start.21
  27.4 14.2 collective-permute-start.4
  34.3 18.4 %collective-permute-start.1 = (bf16[512,512]{1,0:T(8,128)(2,1)S(1)}, bf16[512,512]{1,0:T(8,128)(2,1)S(1)}, u32[]{:S(2)}, u32[]{:S(2)}) collective-permute-start(bf16[512,512]{1,0:T(8,128)(2,1)S(1)} %get-tuple-element.177), channel_id=1, source_target_pairs={{0,2},{1,3},{2,0},{3,1},{4,6},{5,7},{6,4},{7,5},{8,10},{9,11},{10,... | collective-permute-start | bytes 1572872 | tf_op jit(solution)/shard_map/ppermute | solution.py:11
  42.7 11.8 collective-permute-start.5
  52.8 14.3 collective-permute-start.2
  54.5 26.8 %collective-permute-start.6 = (bf16[512,512]{1,0:T(8,128)(2,1)S(1)}, bf16[512,512]{1,0:T(8,128)(2,1)S(1)}, u32[]{:S(2)}, u32[]{:S(2)}) collective-permute-start(bf16[512,512]{1,0:T(8,128)(2,1)S(1)} %broadcast_select_fusion.6), channel_id=1, source_target_pairs={{0,8},{1,9},{2,10},{3,11},{4,12},{5,13},{6,14},{7,15},{8,0},{9,1},... | collective-permute-start | bytes 1572872 | tf_op jit(solution)/shard_map/ppermute | solution.py:11
  67.9 612.8 %collective-permute-start.3 = (bf16[512,512]{1,0:T(8,128)(2,1)}, bf16[512,512]{1,0:T(8,128)(2,1)}, u32[]{:S(2)}, u32[]{:S(2)}) collective-permute-start(bf16[512,512]{1,0:T(8,128)(2,1)} %broadcast_select_fusion.13), channel_id=1, source_target_pairs={{0,8},{1,9},{2,10},{3,11},{4,12},{5,13},{6,14},{7,15},{8,0},{9,1},... | collective-permute-start | bytes 1572872 | tf_op jit(solution)/shard_map/ppermute | solution.py:11
  148.6 4.3 copy-start.15
  223.2 4.3 copy-start.15
  297.7 4.3 copy-start.15
  372.2 4.3 copy-start.15
  446.7 4.3 copy-start.15
  1048.1 4.3 copy-start.17
  1197.3 4.3 copy-start.17
  1283.3 60.8 %copy-start.1 = (f32[1280,512]{1,0:T(8,128)S(1)}, f32[1280,512]{1,0:T(8,128)}, u32[]{:S(2)}) copy-start(f32[1280,512]{1,0:T(8,128)} %get-tuple-element.112) | copy-start | bytes 7864324
  1287.4 56.7 %copy-start.19 = (pred[1024]{0:T(1024)(128)(4,1)S(1)}, pred[1024]{0:T(1024)(128)(4,1)}, u32[]{:S(2)}) copy-start(pred[1024]{0:T(1024)(128)(4,1)} %copy-done.18) | copy-start | bytes 3076
  1342.4 4.9 copy-start.13
  1342.4 12.4 collective-permute-start.11
  1342.9 23.3 %collective-permute-start.7 = (bf16[512,512]{1,0:T(8,128)(2,1)}, bf16[512,512]{1,0:T(8,128)(2,1)}, u32[]{:S(2)}, u32[]{:S(2)}) collective-permute-start(bf16[512,512]{1,0:T(8,128)(2,1)} %get-tuple-element.160), channel_id=1, source_target_pairs={{0,1},{1,0},{2,3},{3,2},{4,5},{5,4},{6,7},{7,6},{8,9},{9,8},{10,11... | collective-permute-start | bytes 1572872 | tf_op jit(solution)/shard_map/ppermute | solution.py:11
  1354.9 27.5 %collective-permute-start.12 = (bf16[512,512]{1,0:T(8,128)(2,1)S(1)}, bf16[512,512]{1,0:T(8,128)(2,1)}, u32[]{:S(2)}, u32[]{:S(2)}) collective-permute-start(bf16[512,512]{1,0:T(8,128)(2,1)S(1)} %broadcast_select_fusion.1), channel_id=1, source_target_pairs={{0,2},{1,3},{2,0},{3,1},{4,6},{5,7},{6,4},{7,5},{8,10},{9,11},{10,... | collective-permute-start | bytes 1572872 | tf_op jit(solution)/shard_map/ppermute | solution.py:11
  1357.6 196.0 %all-to-all-start = ((f32[16,64,512]{2,1,0:T(8,128)}), f32[16,64,512]{2,1,0:T(8,128)}, u32[]{:S(2)}, u32[]{:S(2)}) async-start(f32[16,64,512]{2,1,0:T(8,128)} %bitcast.189), calls=%async_computation | async-start | bytes 4194304 | tf_op jit(solution)/shard_map/all_to_all | solution.py:126
  1362.0 188.3 %all-reduce.4.cloned.1.call-start = ((), (), s32[]{:S(2)}) async-start(), calls=%async_computation.1 | async-start | bytes 4194304 | tf_op jit(solution)/shard_map/psum | solution.py:120
  1368.1 48.6 %collective-permute-start.8 = (bf16[512,512]{1,0:T(8,128)(2,1)}, bf16[512,512]{1,0:T(8,128)(2,1)}, u32[]{:S(2)}, u32[]{:S(2)}) collective-permute-start(bf16[512,512]{1,0:T(8,128)(2,1)} %broadcast_select_fusion.8), channel_id=1, source_target_pairs={{0,2},{1,3},{2,0},{3,1},{4,6},{5,7},{6,4},{7,5},{8,10},{9,11},{10,... | collective-permute-start | bytes 1572872 | tf_op jit(solution)/shard_map/ppermute | solution.py:11
  1383.5 34.5 %collective-permute-start.13 = (bf16[512,512]{1,0:T(8,128)(2,1)S(1)}, bf16[512,512]{1,0:T(8,128)(2,1)S(1)}, u32[]{:S(2)}, u32[]{:S(2)}) collective-permute-start(bf16[512,512]{1,0:T(8,128)(2,1)S(1)} %broadcast_select_fusion.3), channel_id=1, source_target_pairs={{0,4},{1,5},{2,6},{3,7},{4,0},{5,1},{6,2},{7,3},{8,12},{9,13},{10,... | collective-permute-start | bytes 1572872 | tf_op jit(solution)/shard_map/ppermute | solution.py:11
  1383.6 166.8 %copy-start.11 = (bf16[1024,512]{1,0:T(8,128)(2,1)S(1)}, bf16[1024,512]{1,0:T(8,128)(2,1)}, u32[]{:S(2)}) copy-start(bf16[1024,512]{1,0:T(8,128)(2,1)} %param.16) | copy-start | bytes 3145732
  1417.8 12.8 collective-permute-start.9
  1418.1 144.8 %collective-permute-start.14 = (bf16[512,512]{1,0:T(8,128)(2,1)S(1)}, bf16[512,512]{1,0:T(8,128)(2,1)S(1)}, u32[]{:S(2)}, u32[]{:S(2)}) collective-permute-start(bf16[512,512]{1,0:T(8,128)(2,1)S(1)} %broadcast_select_fusion.5), channel_id=1, source_target_pairs={{0,8},{1,9},{2,10},{3,11},{4,12},{5,13},{6,14},{7,15},{8,0},{9,1},... | collective-permute-start | bytes 1572872 | tf_op jit(solution)/shard_map/ppermute | solution.py:11
  1430.6 132.3 %collective-permute-start.10 = (bf16[512,512]{1,0:T(8,128)(2,1)S(1)}, bf16[512,512]{1,0:T(8,128)(2,1)S(1)}, u32[]{:S(2)}, u32[]{:S(2)}) collective-permute-start(bf16[512,512]{1,0:T(8,128)(2,1)S(1)} %broadcast_select_fusion.12), channel_id=1, source_target_pairs={{0,8},{1,9},{2,10},{3,11},{4,12},{5,13},{6,14},{7,15},{8,0},{9,1},... | collective-permute-start | bytes 1572872 | tf_op jit(solution)/shard_map/ppermute | solution.py:11
  1553.6 9.3 copy-start.12
  (77 other events, 190.8 us)
Sparse Core Ops, SparseCore 0:
  1383.7 166.5 all-reduce.3
where the time goes:
time: 1590 us; the launch traced here: 1570 us
  other arithmetic  718 us (45%)
  local copies, waits for them, and re-layouts  378 us (24%)
  waiting for transfers between devices  211 us (13%)
  matrix products  161 us (10%)
  blocking collectives  55 us (3%)
  starting transfers between devices  27.6 us (2%)
  between operations  20.1 us (1%)
    scatter-add x16, other arithmetic, one_group(): slot_grad.at[code_group.reshape(-1)].add(source_grad.reshape(-1, width))  263 us
    scatter-add x16, other arithmetic, one_group(): context_grad.at[row_group.reshape(-1)]  261 us
    gather x16, local copies, waits for them, and re-layouts, one_group(): positive = ctx_panel[row_group]  147 us
    gather x16, local copies, waits for them, and re-layouts, one_group(): sources = slot_table[code_group]  147 us
    psum x1, waiting for transfers between devices, body(): hot_summed = hot_summed + lax.psum(hot_local, ('row', 'col'))  120 us
    scatter-add x16, other arithmetic, one_group(): tile_grad.at[tile_group]  97.7 us
    ppermute x15, waiting for transfers between devices, swapped(): lax.ppermute(x, axis, [(i, i ^ 1 << distance) for i in range(lax.axis_siz...  90.9 us
    dot_general x16, matrix products, one_group(): jnp.einsum('gij,gid->gjd', neg_grad, sources, preferred_element_type=jnp....  68.6 us
  transfers between devices with their start and end apart: 17, of which 9 were waited for; matrix products, arithmetic and copies ran while one was open for 40% of the time, Pallas kernels for 0%

commit v1 on v0

v1 whole, which is shorter than its diff:
```python
import functools

import jax
import jax.numpy as jnp
import numpy as np
from jax import lax
from jax.experimental import pallas as pl
from jax.experimental.pallas import tpu as pltpu
from jax.sharding import Mesh, PartitionSpec as P

NEG_WEIGHT = 0.0625
LEARN_RATE = 0.25

D = 512
BLOCK = 128
HOT = 1024
LHOT = 256
CAP = 64
VS = 256
CR = 512
NX = 4
NCORE = 2
NCOL = 16
NBLK = 128
SLOTS = LHOT + NCOL * CAP
HALF_SLOTS = SLOTS // 2
CHUNK = 16
BASE = 4096.0

F32 = jnp.float32
BF16 = jnp.bfloat16
I16 = jnp.int16
NN = (((1,), (0,)), ((), ()))
NT = (((1,), (1,)), ((), ()))
TN = (((0,), (0,)), ((), ()))


def dot(a, b, dims):
    return lax.dot_general(a, b, dims, preferred_element_type=F32)


def params(mib):
    return pltpu.CompilerParams(vmem_limit_bytes=mib * 2**20)


def cost(flops, nbytes):
    return pl.CostEstimate(flops=flops, bytes_accessed=nbytes, transcendentals=0)


def one_hot(rows, ids, weight=None):
    shape = (rows, ids.shape[1])
    index = lax.broadcasted_iota(jnp.int32, shape, 0).astype(I16)
    hit = index == jnp.broadcast_to(ids.astype(I16), shape)
    value = jnp.ones((), BF16) if weight is None else jnp.broadcast_to(weight, shape)
    return jnp.where(hit, value, jnp.zeros((), BF16))


def split(x):
    high = x.astype(BF16)
    return high, (x - high.astype(F32)).astype(BF16)


def count_kernel(episode, tiles, codes, rows, pairs, tile_counts, left, right, left2, right2):
    step = pl.program_id(0)

    @pl.when(step == 0)
    def _():
        pairs[...] = jnp.zeros_like(pairs)
        tile_counts[...] = jnp.zeros_like(tile_counts)

    for n in range(CHUNK):
        at = slice(n * BLOCK, (n + 1) * BLOCK)
        code = codes[n : n + 1, :]
        upper = code >= HALF_SLOTS
        weight = jnp.where(upper, BASE, 1.0).astype(BF16)
        left[:, at] = one_hot(HALF_SLOTS, jnp.where(upper, code - HALF_SLOTS, code), weight)
        right[:, at] = one_hot(CR, rows[n : n + 1, :])
        tile = tiles[episode * NBLK + step * CHUNK + n]
        left2[:, at] = one_hot(48, code >> 5)
        right2[:, at] = one_hot(128, (code & 31) * 4 + tile)
    packed = dot(left[...], right[...], NT)
    high = jnp.floor(packed * (1.0 / BASE))
    pairs[0:HALF_SLOTS] += packed - high * BASE
    pairs[HALF_SLOTS:SLOTS] += high
    tile_counts[...] += dot(left2[...], right2[...], NT)


def edge_counts(episode, src_code, ctx_rows, neg_tiles):
    block = pl.BlockSpec((None, None, None, CHUNK, BLOCK), lambda i, t: (0, 0, episode, i, 0))
    width = CHUNK * BLOCK
    return pl.pallas_call(
        functools.partial(count_kernel, episode),
        out_shape=[
            jax.ShapeDtypeStruct((SLOTS, CR), F32),
            jax.ShapeDtypeStruct((48, 128), F32),
        ],
        grid_spec=pltpu.PrefetchScalarGridSpec(
            num_scalar_prefetch=1,
            grid=(NBLK // CHUNK,),
            in_specs=[block, block],
            out_specs=[
                pl.BlockSpec((SLOTS, CR), lambda i, t: (0, 0)),
                pl.BlockSpec((48, 128), lambda i, t: (0, 0)),
            ],
            scratch_shapes=[
                pltpu.VMEM((HALF_SLOTS, width), BF16),
                pltpu.VMEM((CR, width), BF16),
                pltpu.VMEM((48, width), BF16),
                pltpu.VMEM((128, width), BF16),
            ],
        ),
        compiler_params=params(40),
        cost_estimate=cost(2 * NBLK * BLOCK * HALF_SLOTS * CR, 3 << 20),
        name="edge_counts",
    )(neg_tiles.reshape(-1), src_code, ctx_rows)


def slot_kernel(panel, hot_table, hot_list, cold_ids, out):
    owners = pl.program_id(0)

    @pl.when(owners == 0)
    def _():
        out[...] = dot(one_hot(HOT, hot_list[...]), hot_table[...], TN).astype(BF16)

    @pl.when(owners > 0)
    def _():
        for o in range(4):
            ids = cold_ids[o : o + 1, :]
            rows = dot(one_hot(VS, ids), panel[o * VS : (o + 1) * VS, :], TN)
            out[o * CAP : (o + 1) * CAP, :] = rows.astype(BF16)


def slot_rows(panel, hot_table, hot_list, cold_ids):
    later = lambda i: (jnp.maximum(i - 1, 0), 0)
    return pl.pallas_call(
        slot_kernel,
        out_shape=jax.ShapeDtypeStruct((SLOTS, D), BF16),
        grid=(5,),
        in_specs=[
            pl.BlockSpec((4 * VS, D), later),
            pl.BlockSpec((HOT, D), lambda i: (0, 0)),
            pl.BlockSpec((1, LHOT), lambda i: (0, 0)),
            pl.BlockSpec((None, 4, CAP), lambda i: (jnp.maximum(i - 1, 0), 0, 0)),
        ],
        out_specs=pl.BlockSpec((LHOT, D), lambda i: (i, 0)),
        compiler_params=params(24),
        cost_estimate=cost(1 << 29, 6 << 20),
        name="slot_rows",
    )(panel, hot_table, hot_list, cold_ids.reshape(4, 4, CAP))


def pick_kernel(matching, pieces, out):
    for episode in range(2):
        for reader in range(NCOL):
            partner = matching[episode * NCOL + reader]
            out[reader, episode] = pieces[partner]


def pick_pieces(matching, pieces):
    rows = pieces.shape[1]
    return pl.pallas_call(
        pick_kernel,
        out_shape=jax.ShapeDtypeStruct((NCOL, 2, rows, D), BF16),
        in_specs=[
            pl.BlockSpec(memory_space=pltpu.SMEM),
            pl.BlockSpec(memory_space=pltpu.VMEM),
        ],
        out_specs=pl.BlockSpec(memory_space=pltpu.VMEM),
        compiler_params=params(16),
        cost_estimate=cost(0, 2 << 20),
        name="pick_pieces",
    )(matching.reshape(-1), pieces)


def grad_kernel(
    core, slots, ctx, pairs0, pairs1, counts0, counts1, hot_list, cold, keep, send, ctx_acc, hot_acc
):
    step = pl.program_id(0)

    @pl.when(step == 0)
    def _():
        ctx_acc[...] = jnp.zeros_like(ctx_acc)

    here = slots[...]
    slot_at = step * LHOT + lax.broadcasted_iota(jnp.int32, (LHOT, 48), 0)
    group = ((slot_at >> 5) == lax.broadcasted_iota(jnp.int32, (LHOT, 48), 1)).astype(F32).astype(BF16)
    lane = lax.broadcasted_iota(jnp.int32, (LHOT, 256), 1)
    slot_in = lax.broadcasted_iota(jnp.int32, (LHOT, 256), 0) & 31
    mine = ((lane & 127) >> 2) == slot_in
    pick_row = lax.broadcasted_iota(jnp.int32, (256, CR), 0)
    pick_col = lax.broadcasted_iota(jnp.int32, (256, CR), 1)
    spread = jnp.where(
        (pick_row & 3) == (pick_col >> 7), jnp.where(pick_row >= 128, 128.0, 1.0), 0.0
    ).astype(BF16)
    slot_grad = jnp.zeros((LHOT, D), F32)
    for episode in range(2):
        panel = ctx[:, episode].reshape(CR, D)
        counted = (pairs0, pairs1)[episode][...]
        table = (counts0, counts1)[episode][...]
        upper = jnp.floor(table * (1.0 / 128.0))
        both = jnp.concatenate([table - upper * 128.0, upper], 1).astype(BF16)
        taken = jnp.where(mine, dot(group, both, NN), 0.0).astype(BF16)
        tiled = dot(taken, spread, NN)
        score = dot(here, panel, NT)
        curve = jnp.tanh(0.5 * score)
        negative = (0.5 * NEG_WEIGHT + (0.5 * NEG_WEIGHT) * curve).astype(BF16).astype(F32)
        grad = tiled * negative - counted * (0.5 - 0.5 * curve)
        high, low = split(grad)
        slot_grad += dot(high, panel, NN) + dot(low, panel, NN)
        ctx_acc[episode] += dot(high, here, TN) + dot(low, here, TN)

    @pl.when(step == 0)
    def _():
        high, low = split(slot_grad)
        where_hot = one_hot(HOT, hot_list[...])
        hot_acc[...] = dot(where_hot, high, NN) + dot(where_hot, low, NN)

    @pl.when(step > 0)
    def _():
        cold[...] = slot_grad.astype(BF16)

    @pl.when(step == pl.num_programs(0) - 1)
    def _():
        for half, out in ((core[0], keep), (1 - core[0], send)):
            for x in range(NX):
                hot_at = pl.multiple_of(half * (HOT // 2) + x * 128, 128)
                ctx_at = pl.multiple_of(half * (CR // 2) + x * 64, 64)
                out[x, 0:128] = hot_acc[pl.ds(hot_at, 128)]
                out[x, 128:192] = ctx_acc[0, pl.ds(ctx_at, 64)]
                out[x, 192:256] = ctx_acc[1, pl.ds(ctx_at, 64)]


def gradients(core, slots, ctx, counts, hot_list):
    (pairs0, tiles0), (pairs1, tiles1) = counts
    chunk = pl.BlockSpec((LHOT, CR), lambda i, c: (i, 0))
    whole = lambda *shape: pl.BlockSpec(shape, lambda i, c: (0,) * len(shape))
    part = jax.ShapeDtypeStruct((NX, 256, D), F32)
    return pl.pallas_call(
        grad_kernel,
        out_shape=[jax.ShapeDtypeStruct((NCOL * CAP, D), BF16), part, part],
        grid_spec=pltpu.PrefetchScalarGridSpec(
            num_scalar_prefetch=1,
            grid=(5,),
            in_specs=[
                chunk,
                whole(NCOL, 2, CR // NCOL, D),
                chunk,
                chunk,
                whole(48, 128),
                whole(48, 128),
                whole(1, LHOT),
            ],
            out_specs=[
                pl.BlockSpec((LHOT, D), lambda i, c: (jnp.maximum(i - 1, 0), 0)),
                whole(NX, 256, D),
                whole(NX, 256, D),
            ],
            scratch_shapes=[pltpu.VMEM((2, CR, D), F32), pltpu.VMEM((HOT, D), F32)],
        ),
        compiler_params=params(48),
        cost_estimate=cost(6 << 30, 12 << 20),
        name="gradients",
    )(core, slots, ctx, pairs0, pairs1, tiles0, tiles1, hot_list)


def x_sum_kernel(parts, out):
    total = parts[0].astype(F32)
    for x in range(1, NX):
        total += parts[x].astype(F32)
    for j in range(NCOL):
        pair = jnp.concatenate([total[j * 8 : j * 8 + 8], total[128 + j * 8 : 136 + j * 8]], 0)
        out[j] = pair.astype(BF16)


def x_sum(parts):
    return pl.pallas_call(
        x_sum_kernel,
        out_shape=jax.ShapeDtypeStruct((NCOL, 16, D), BF16),
        compiler_params=params(16),
        cost_estimate=cost(1 << 20, 2 << 20),
        name="x_sum",
    )(parts)


def col_sum_kernel(partner, parts, out):
    hot = parts[0].astype(F32)[0:8]
    for c in range(1, NCOL):
        hot += parts[c].astype(F32)[0:8]
    for q in range(NCOL):
        step = parts[partner[q]].astype(F32)[8:16]
        pair = jnp.concatenate([hot, step], 0).astype(BF16)
        for x in range(NX):
            out[x, q] = pair


def col_sum(partner, parts):
    return pl.pallas_call(
        col_sum_kernel,
        out_shape=jax.ShapeDtypeStruct((NX, NCOL, 16, D), BF16),
        in_specs=[
            pl.BlockSpec(memory_space=pltpu.SMEM),
            pl.BlockSpec(memory_space=pltpu.VMEM),
        ],
        out_specs=pl.BlockSpec(memory_space=pltpu.VMEM),
        compiler_params=params(16),
        cost_estimate=cost(1 << 20, 2 << 20),
        name="col_sum",
    )(partner, parts)


def finish_kernel(core, own, other, hot_table, context, hot_out, context_out):
    for from_other, parts in ((0, own), (1, other)):
        half = core[0] if from_other == 0 else 1 - core[0]
        for x in range(NX):
            hot_at = pl.multiple_of(half * (HOT // 2) + x * 128, 128)
            ctx_at = pl.multiple_of(half * (CR // 2) + x * 64, 64)
            first = [parts[x, j].astype(F32) for j in range(NCOL)]
            hot = jnp.concatenate([p[0:8] for p in first], 0)
            step = jnp.concatenate([first[j][8:16] + first[j + 8][8:16] for j in range(8)], 0)
            hot_rows = hot_table[pl.ds(hot_at, 128)].astype(F32)
            hot_out[pl.ds(hot_at, 128)] = hot_rows - LEARN_RATE * hot
            ctx_rows = context[pl.ds(ctx_at, 64)].astype(F32)
            context_out[pl.ds(ctx_at, 64)] = ctx_rows - LEARN_RATE * step


def finish(core, own, other, hot_table, context):
    vmem = pl.BlockSpec(memory_space=pltpu.VMEM)
    return pl.pallas_call(
        finish_kernel,
        out_shape=[jax.ShapeDtypeStruct((HOT, D), F32), jax.ShapeDtypeStruct((CR, D), F32)],
        in_specs=[pl.BlockSpec(memory_space=pltpu.SMEM), vmem, vmem, vmem, vmem],
        out_specs=[vmem, vmem],
        compiler_params=params(24),
        cost_estimate=cost(1 << 20, 7 << 20),
        name="finish",
    )(core, own, other, hot_table, context)


def vertex_kernel(col, ids, received, panel, out):
    total = jnp.zeros((VS, D), F32)
    for n in range(8):
        where_row = one_hot(VS, ids[n : n + 1, :])
        total += dot(where_row, received[n * 128 : (n + 1) * 128, :], NN)
    out[...] = panel[...].astype(F32) - LEARN_RATE * total


def vertex_rows(col, ids, received, panel):
    return pl.pallas_call(
        vertex_kernel,
        out_shape=jax.ShapeDtypeStruct((VS, D), F32),
        grid_spec=pltpu.PrefetchScalarGridSpec(
            num_scalar_prefetch=1,
            grid=(1,),
            in_specs=[
                pl.BlockSpec((8, 128), lambda i, c: (0, 0)),
                pl.BlockSpec((NCOL * CAP, D), lambda i, c: (0, 0)),
                pl.BlockSpec((VS, D), lambda i, c: (c[0], 0)),
            ],
            out_specs=pl.BlockSpec((VS, D), lambda i, c: (0, 0)),
        ),
        compiler_params=params(16),
        cost_estimate=cost(1 << 28, 2 << 20),
        name="vertex_rows",
    )(col, ids, received, panel)


def all_to_all(x, axes):
    return lax.all_to_all(x, axes, 0, 0, tiled=True)


def body(
    vertex_panel,
    context_panel,
    hot_table,
    matching,
    hot_map,
    cold_list,
    cold_count,
    src_code,
    ctx_rows,
    neg_tiles,
):
    col_index = lax.axis_index("col")
    core = lax.axis_index("core").astype(jnp.int32)[None]
    col = col_index.astype(jnp.int32)[None]
    hot_list = hot_map[0]
    live = jnp.arange(CAP, dtype=jnp.int32) < cold_count[0][..., None]
    ids = jnp.where(live, cold_list[0], -1)
    own_ids = lax.dynamic_index_in_dim(ids, col_index, 0, keepdims=False)
    sender_ids = lax.dynamic_index_in_dim(ids, col_index, 1, keepdims=False).reshape(8, 128)

    pieces = all_to_all(context_panel.reshape(NCOL, CR // NCOL, D), "col")
    counts = [edge_counts(0, src_code, ctx_rows, neg_tiles)]
    ctx = all_to_all(pick_pieces(matching, pieces), "col")
    counts.append(edge_counts(1, src_code, ctx_rows, neg_tiles))
    slots = slot_rows(vertex_panel, hot_table, hot_list, own_ids)

    cold, keep, send = gradients(core, slots, ctx, counts, hot_list)
    arrived = lax.ppermute(send, "core", [(0, 1), (1, 0)])
    received = all_to_all(cold.reshape(NCOL, CAP, D), "col").reshape(NCOL * CAP, D)
    parts = all_to_all((keep + arrived).astype(BF16), "x")
    parts = all_to_all(x_sum(parts), "col")
    episode = (col_index >= NCOL // 2).astype(jnp.int32)
    partner = lax.dynamic_index_in_dim(matching, episode, 0, keepdims=False)
    parts = col_sum(partner, parts).reshape(NX * NCOL, 16, D)
    own = all_to_all(parts, ("x", "col")).reshape(NX, NCOL, 16, D)
    other = lax.ppermute(own, "core", [(0, 1), (1, 0)])
    hot_new, context_new = finish(core, own, other, hot_table, context_panel)
    vertex_new = vertex_rows(col, sender_ids, received, vertex_panel)
    return (vertex_new, context_new, hot_new)


def solution(mesh):
    split_mesh = Mesh(mesh.devices.reshape(NX, NCORE, NCOL), ("x", "core", "col"))
    row = ("x", "core")
    in_specs = (
        P(row, None),
        P("col", None),
        P(),
        P(),
        P(row, "col", None),
        P(row, None, None, None),
        P(row, None, None),
        P(row, "col", None, None, None),
        P(row, "col", None, None, None),
        P(row, "col", None, None),
    )
    out_specs = (P(("x", "core", "col"), None), P("col", None), P())
    return jax.shard_map(
        body, mesh=split_mesh, in_specs=in_specs, out_specs=out_specs, check_vma=False
    )
```

time: 1590 us -> 174 us (0.11); the launches traced: 1570 us -> 174 us
  other arithmetic: 718 us -> 0.64 us
  local copies, waits for them, and re-layouts: 378 us -> 10.1 us
  waiting for transfers between devices: 211 us -> 30.6 us
  matrix products: 161 us -> 0 us
  Pallas kernels: 0 us -> 62 us
  between operations: 20.1 us -> 0.87 us
  blocking collectives: 55 us -> 38.1 us
    scatter-add x51 -> x0, other arithmetic: 637 us -> none  [the longest x16 263 us: one_group(): slot_grad.at[code_group.reshape(-1)].add(source_grad.reshape(-1, width))]
    gather x50 -> x0, local copies, waits for them, and re-layouts: 334 us -> none  [the longest x16 147 us: one_group(): positive = ctx_panel[row_group]]
    dot_general x48 -> x0, matrix products: 161 us -> none  [the longest x16 68.6 us: one_group(): jnp.einsum('gij,gid->gjd', neg_grad, sources, preferred_element_type=jnp....]
    psum x1 -> x0, waiting for transfers between devices: 120 us -> none  [body(): hot_summed = hot_summed + lax.psum(hot_local, ('row', 'col'))]
    ppermute x15 -> x2, waiting for transfers between devices: 90.9 us -> 4 us  [the longest x1 4 us: body(): arrived = lax.ppermute(send, 'core', [(0, 1), (1, 0)])]
    pallas_call x0 -> x9, Pallas kernels: none -> 62 us  [the longest x2 36.5 us: edge_counts(): pl.pallas_call(functools.partial(count_kernel, episode), out_shape=[jax.S...]
    psum x1 -> x0, blocking collectives: 55 us -> none  [body(): summed = lax.psum(context_grad, 'row').astype(jnp.bfloat16)]
    all_to_all x0 -> x2, blocking collectives: none -> 38.1 us  [all_to_all(): return lax.all_to_all(x, axes, 0, 0, tiled=True)]
  transfers between devices with their start and end apart: 17 -> 6, of which waited for: 9 -> 3; matrix products, arithmetic and copies ran while one was open for 40% -> 0% of each run, Pallas kernels for 0% -> 23%
where the time goes in v1:
time: 174 us
  Pallas kernels  62 us (36%)
  blocking collectives  38.1 us (22%)
  starting transfers between devices  31.2 us (18%)
  waiting for transfers between devices  30.6 us (18%)
  local copies, waits for them, and re-layouts  10.1 us (6%)
    all_to_all x2, blocking collectives, all_to_all(): return lax.all_to_all(x, axes, 0, 0, tiled=True)  38.1 us
    pallas_call x2, Pallas kernels, edge_counts(): pl.pallas_call(functools.partial(count_kernel, episode), out_shape=[jax.S...  36.5 us
    all_to_all x4, waiting for transfers between devices, all_to_all(): return lax.all_to_all(x, axes, 0, 0, tiled=True)  26.6 us
    all_to_all x4, starting transfers between devices, all_to_all(): return lax.all_to_all(x, axes, 0, 0, tiled=True)  25.8 us
    pallas_call x1, Pallas kernels, gradients(): pl.pallas_call(grad_kernel, out_shape=[jax.ShapeDtypeStruct((NCOL * CAP,...  15.9 us
    unnamed x34, local copies, waits for them, and re-layouts  9.94 us
    ppermute x1, waiting for transfers between devices, body(): arrived = lax.ppermute(send, 'core', [(0, 1), (1, 0)])  4 us
    ppermute x1, starting transfers between devices, body(): other = lax.ppermute(own, 'core', [(0, 1), (1, 0)])  3.87 us
  transfers between devices with their start and end apart: 6, of which 3 were waited for; matrix products, arithmetic and copies ran while one was open for 0% of the time, Pallas kernels for 23%

profile of v1, /device:TPU:1, one launch (start us, length us, event | category | flops | bytes accessed | tf_op | source)
XLA Modules:
  0.0 173.6 jit_solution(11281392381805640846)
XLA Ops:
  0.6 8.6 %all-to-all-start = ((bf16[16,32,512]{2,1,0:T(8,128)(2,1)}), bf16[16,32,512]{2,1,0:T(8,128)(2,1)S(1)}, u32[]{:S(2)}, u32[]{:S(2)}) async-start(bf16[16,32,512]{2,1,0:T(8,128)(2,1)} %bitcast.19), calls=%async_computation | async-start | bytes 1048576 | tf_op jit(solution)/shard_map/all_to_all | solution.py:368
  9.2 0.0 copy-start.6
  9.3 0.9 copy-done.6
  10.2 0.9 copy-done.8
  11.1 0.7 copy-done.10
  11.8 18.3 %edge_counts.2 = (f32[1280,512]{1,0:T(8,128)S(1)}, f32[48,128]{1,0:T(8,128)S(1)}) custom-call(s32[256]{0:T(256)S(1)} %bitcast.24, s32[1,1,2,128,128]{4,3,2,1,0:T(8,128)S(1)} %copy-done.6, s32[1,1,2,128,128]{4,3,2,1,0:T(8,128)S(1)} %copy-done.8), custom_call_target="tpu_custom_call" | custom-call | flops 10737418240 | bytes 3145728 | tf_op jit(solution)/shard_map/edge_counts/pallas_call | solution.py:91
  30.0 1.5 copy-done.12
  31.5 0.1 reshape.39.matching
  31.6 0.1 bitcast_select_fusion
  31.8 2.2 %copy-done = bf16[4096,512]{1,0:T(8,128)(2,1)S(1)} copy-done((bf16[4096,512]{1,0:T(8,128)(2,1)S(1)}, bf16[4096,512]{1,0:T(8,128)(2,1)}, u32[]{:S(2)}) %copy-start) | copy-done | bytes 4194328
  34.0 1.8 %slot_rows.1.slots = bf16[1280,512]{1,0:T(8,128)(2,1)S(1)} custom-call(bf16[4096,512]{1,0:T(8,128)(2,1)S(1)} %copy-done, bf16[1024,512]{1,0:T(8,128)(2,1)S(1)} %copy-done.2, s32[1,256]{1,0:T(1,128)S(1)} %bitcast.22, s32[4,4,64]{2,1,0:T(4,128)S(1)} %bitcast.21), custom_call_target="tpu_custom_call" | custom-call | flops 536870912 | bytes 6291456 | tf_op jit(solution)/shard_map/slot_rows/pallas_call | solution.py:135
  35.8 1.6 pick_pieces.1
  37.4 6.7 %all-to-all-start.1 = ((bf16[16,2,32,512]{3,2,1,0:T(8,128)(2,1)}), bf16[16,2,32,512]{3,2,1,0:T(8,128)(2,1)}, u32[]{:S(2)}, u32[]{:S(2)}) async-start(bf16[16,2,32,512]{3,2,1,0:T(8,128)(2,1)} %pick_pieces.1), calls=%async_computation.1 | async-start | bytes 2097152 | tf_op jit(solution)/shard_map/all_to_all | solution.py:368
  44.2 18.3 %edge_counts.3 = (f32[1280,512]{1,0:T(8,128)S(1)}, f32[48,128]{1,0:T(8,128)S(1)}) custom-call(s32[256]{0:T(256)S(1)} %bitcast.25, s32[1,1,2,128,128]{4,3,2,1,0:T(8,128)S(1)} %copy-done.7, s32[1,1,2,128,128]{4,3,2,1,0:T(8,128)S(1)} %copy-done.9), custom_call_target="tpu_custom_call" | custom-call | flops 10737418240 | bytes 3145728 | tf_op jit(solution)/shard_map/edge_counts/pallas_call | solution.py:91
  62.4 1.5 copy-done.13
  64.0 15.9 %gradients.1 = (bf16[1024,512]{1,0:T(8,128)(2,1)S(1)}, f32[4,256,512]{2,1,0:T(8,128)S(1)}, f32[4,256,512]{2,1,0:T(8,128)}) custom-call(s32[1]{0:T(128)} %bitcast.3.core, bf16[1280,512]{1,0:T(8,128)(2,1)S(1)} %slot_rows.1.slots, bf16[16,2,32,512]{3,2,1,0:T(8,128)(2,1)} %all-to-all-done.1.ctx, f32[1280,512]{1,0:T(8,128)} %copy-done.12, ...), custom_call_target="tpu_custom_call" | custom-call | flops 6442450944 | bytes 12582912 | tf_op jit(solution)/shard_map/gradients/pallas_call | solution.py:238
  79.8 1.5 collective-permute-start
  81.4 4.0 %collective-permute-done = f32[4,256,512]{2,1,0:T(8,128)S(1)} collective-permute-done((f32[4,256,512]{2,1,0:T(8,128)}, f32[4,256,512]{2,1,0:T(8,128)S(1)}, u32[]{:S(2)}, u32[]{:S(2)}) %collective-permute-start) | collective-permute-done | bytes 2097184 | tf_op jit(solution)/shard_map/ppermute | solution.py:399
  85.4 0.5 add_convert_fusion
  85.9 18.1 %all_to_all.30.parts = bf16[4,256,512]{2,1,0:T(8,128)(2,1)S(1)} all-to-all(bf16[4,256,512]{2,1,0:T(8,128)(2,1)S(1)} %add_convert_fusion), channel_id=1, replica_groups=mesh['x'=4,'core'=2,'col'=16] {'x'}, dimensions={0} | all-to-all | bytes 2097152 | tf_op jit(solution)/shard_map/all_to_all | solution.py:368
  104.0 0.8 x_sum.1
  104.8 6.9 %all-to-all-start.4 = ((bf16[16,16,512]{2,1,0:T(8,128)(2,1)}), bf16[16,16,512]{2,1,0:T(8,128)(2,1)S(1)}, u32[]{:S(2)}, u32[]{:S(2)}) async-start(bf16[16,16,512]{2,1,0:T(8,128)(2,1)} %x_sum.1), calls=%async_computation.4 | async-start | bytes 524288 | tf_op jit(solution)/shard_map/all_to_all | solution.py:368
  111.7 7.5 %all-to-all-done.4.parts = bf16[16,16,512]{2,1,0:T(8,128)(2,1)S(1)} async-done(((bf16[16,16,512]{2,1,0:T(8,128)(2,1)}), bf16[16,16,512]{2,1,0:T(8,128)(2,1)S(1)}, u32[]{:S(2)}, u32[]{:S(2)}) %all-to-all-start.4) | async-done | bytes 262176 | tf_op jit(solution)/shard_map/all_to_all | solution.py:368
  119.2 0.6 col_sum.1
  119.9 20.0 %all_to_all.31 = bf16[64,16,512]{2,1,0:T(8,128)(2,1)S(1)} all-to-all(bf16[64,16,512]{2,1,0:T(8,128)(2,1)S(1)} %bitcast.15), channel_id=1, replica_groups=mesh['x'=4,'core'=2,'col'=16] {'x','col'}, dimensions={0} | all-to-all | bytes 2097152 | tf_op jit(solution)/shard_map/all_to_all | solution.py:368
  139.9 3.9 %collective-permute-start.1 = (bf16[4,16,16,512]{3,2,1,0:T(8,128)(2,1)S(1)}, bf16[4,16,16,512]{3,2,1,0:T(8,128)(2,1)}, u32[]{:S(2)}, u32[]{:S(2)}) collective-permute-start(bf16[4,16,16,512]{3,2,1,0:T(8,128)(2,1)S(1)} %bitcast.16), channel_id=1, source_target_pairs={{0,16},{16,0},{1,17},{17,1},{2,18},{18,2},{3,19},{19,3},{4,20},{20... | collective-permute-start | bytes 3145736 | tf_op jit(solution)/shard_map/ppermute | solution.py:407
  143.8 3.7 %all-to-all-start.2 = ((bf16[16,64,512]{2,1,0:T(8,128)(2,1)}), bf16[16,64,512]{2,1,0:T(8,128)(2,1)S(1)}, u32[]{:S(2)}, u32[]{:S(2)}) async-start(bf16[16,64,512]{2,1,0:T(8,128)(2,1)} %bitcast.20), calls=%async_computation.2 | async-start | bytes 2097152 | tf_op jit(solution)/shard_map/all_to_all | solution.py:368
  147.5 0.1 reshape.37.ids
  147.6 19.1 %all-to-all-done.2 = bf16[16,64,512]{2,1,0:T(8,128)(2,1)S(1)} async-done(((bf16[16,64,512]{2,1,0:T(8,128)(2,1)}), bf16[16,64,512]{2,1,0:T(8,128)(2,1)S(1)}, u32[]{:S(2)}, u32[]{:S(2)}) %all-to-all-start.2) | async-done | bytes 1048608 | tf_op jit(solution)/shard_map/all_to_all | solution.py:368
  166.7 2.2 %copy-done.1 = bf16[4096,512]{1,0:T(8,128)(2,1)S(1)} copy-done((bf16[4096,512]{1,0:T(8,128)(2,1)S(1)}, bf16[4096,512]{1,0:T(8,128)(2,1)}, u32[]{:S(2)}) %copy-start.1) | copy-done | bytes 4194328
  168.9 1.5 vertex_rows.1
  170.3 3.3 %finish.1 = (f32[1024,512]{1,0:T(8,128)}, f32[512,512]{1,0:T(8,128)}) custom-call(s32[1]{0:T(128)} %bitcast.3.core, bf16[4,16,16,512]{3,2,1,0:T(8,128)(2,1)S(1)} %bitcast.17, bf16[4,16,16,512]{3,2,1,0:T(8,128)(2,1)} %collective-permute-done.1.other, bf16[1024,512]{1,0:T(8,128)(2,1)S(1)} %copy-done.2, bf16[512,512]{1,0:T(8,128)(2,1)S(1)} %copy-done.3), custom_call_target="tpu_custom_call" | custom-call | flops 1048576 | bytes 7340032 | tf_op jit(solution)/shard_map/finish/pallas_call | solution.py:328
  (32 shorter events, 0.1 us)
Async XLA Ops:
  0.6 35.2 %all-to-all-start = ((bf16[16,32,512]{2,1,0:T(8,128)(2,1)}), bf16[16,32,512]{2,1,0:T(8,128)(2,1)S(1)}, u32[]{:S(2)}, u32[]{:S(2)}) async-start(bf16[16,32,512]{2,1,0:T(8,128)(2,1)} %bitcast.19), calls=%async_computation | async-start | bytes 1048576 | tf_op jit(solution)/shard_map/all_to_all | solution.py:368
  9.2 0.9 copy-start.6
  10.2 0.9 copy-start.8
  11.1 0.7 copy-start.10
  11.7 19.8 %copy-start.16 = (s32[2,16]{1,0:T(2,128)S(1)}, s32[2,16]{1,0:T(2,128)}, u32[]{:S(2)}) copy-start(s32[2,16]{1,0:T(2,128)} %param.13) | copy-start | bytes 388
  11.7 19.9 %copy-start.14 = (s32[1,16,16,64]{3,2,1,0:T(8,128)S(1)}, s32[1,16,16,64]{3,2,1,0:T(8,128)}, u32[]{:S(2)}) copy-start(s32[1,16,16,64]{3,2,1,0:T(8,128)} %param.15) | copy-start | bytes 196612
  11.7 19.9 %copy-start.15 = (s32[1,16,16]{2,1,0:T(8,128)S(1)}, s32[1,16,16]{2,1,0:T(8,128)}, u32[]{:S(2)}) copy-start(s32[1,16,16]{2,1,0:T(8,128)} %param.16) | copy-start | bytes 3076
  11.7 20.0 %copy-start.2 = (bf16[1024,512]{1,0:T(8,128)(2,1)S(1)}, bf16[1024,512]{1,0:T(8,128)(2,1)}, u32[]{:S(2)}) copy-start(bf16[1024,512]{1,0:T(8,128)(2,1)} %hot_table.3) | copy-start | bytes 3145732
  11.7 20.0 %copy-start.5 = (s32[1,1,256]{2,1,0:T(1,128)S(1)}, s32[1,1,256]{2,1,0:T(1,128)}, u32[]{:S(2)}) copy-start(s32[1,1,256]{2,1,0:T(1,128)} %param.14) | copy-start | bytes 3076
  30.0 1.5 copy-start.12
  31.8 2.2 %copy-start = (bf16[4096,512]{1,0:T(8,128)(2,1)S(1)}, bf16[4096,512]{1,0:T(8,128)(2,1)}, u32[]{:S(2)}) copy-start(bf16[4096,512]{1,0:T(8,128)(2,1)} %panel.3) | copy-start | bytes 12582916
  35.8 8.3 %copy-start.7 = (s32[1,1,2,128,128]{4,3,2,1,0:T(8,128)S(1)}, s32[1,1,2,128,128]{4,3,2,1,0:T(8,128)}, u32[]{:S(2)}) copy-start(s32[1,1,2,128,128]{4,3,2,1,0:T(8,128)} %codes.3) | copy-start | bytes 393220
  35.8 8.3 %copy-start.9 = (s32[1,1,2,128,128]{4,3,2,1,0:T(8,128)S(1)}, s32[1,1,2,128,128]{4,3,2,1,0:T(8,128)}, u32[]{:S(2)}) copy-start(s32[1,1,2,128,128]{4,3,2,1,0:T(8,128)} %rows.3) | copy-start | bytes 393220
  35.8 8.3 %copy-start.11 = (s32[1,1,2,128]{3,2,1,0:T(2,128)S(1)}, s32[1,1,2,128]{3,2,1,0:T(2,128)}, u32[]{:S(2)}) copy-start(s32[1,1,2,128]{3,2,1,0:T(2,128)} %param.19) | copy-start | bytes 3076
  37.4 26.6 %all-to-all-start.1 = ((bf16[16,2,32,512]{3,2,1,0:T(8,128)(2,1)}), bf16[16,2,32,512]{3,2,1,0:T(8,128)(2,1)}, u32[]{:S(2)}, u32[]{:S(2)}) async-start(bf16[16,2,32,512]{3,2,1,0:T(8,128)(2,1)} %pick_pieces.1), calls=%async_computation.1 | async-start | bytes 2097152 | tf_op jit(solution)/shard_map/all_to_all | solution.py:368
  62.4 1.6 copy-start.13
  79.8 6.1 %copy-start.4 = (bf16[1024,512]{1,0:T(8,128)(2,1)}, bf16[1024,512]{1,0:T(8,128)(2,1)S(1)}, u32[]{:S(2)}) copy-start(bf16[1024,512]{1,0:T(8,128)(2,1)S(1)} %get-tuple-element.16) | copy-start | bytes 3145732
  79.8 5.5 %collective-permute-start = (f32[4,256,512]{2,1,0:T(8,128)}, f32[4,256,512]{2,1,0:T(8,128)S(1)}, u32[]{:S(2)}, u32[]{:S(2)}) collective-permute-start(f32[4,256,512]{2,1,0:T(8,128)} %get-tuple-element.18), channel_id=1, source_target_pairs={{0,16},{16,0},{1,17},{17,1},{2,18},{18,2},{3,19},{19,3},{4,20},{20... | collective-permute-start | bytes 6291464 | tf_op jit(solution)/shard_map/ppermute | solution.py:399
  104.8 14.4 %all-to-all-start.4 = ((bf16[16,16,512]{2,1,0:T(8,128)(2,1)}), bf16[16,16,512]{2,1,0:T(8,128)(2,1)S(1)}, u32[]{:S(2)}, u32[]{:S(2)}) async-start(bf16[16,16,512]{2,1,0:T(8,128)(2,1)} %x_sum.1), calls=%async_computation.4 | async-start | bytes 524288 | tf_op jit(solution)/shard_map/all_to_all | solution.py:368
  139.9 30.4 %collective-permute-start.1 = (bf16[4,16,16,512]{3,2,1,0:T(8,128)(2,1)S(1)}, bf16[4,16,16,512]{3,2,1,0:T(8,128)(2,1)}, u32[]{:S(2)}, u32[]{:S(2)}) collective-permute-start(bf16[4,16,16,512]{3,2,1,0:T(8,128)(2,1)S(1)} %bitcast.16), channel_id=1, source_target_pairs={{0,16},{16,0},{1,17},{17,1},{2,18},{18,2},{3,19},{19,3},{4,20},{20... | collective-permute-start | bytes 3145736 | tf_op jit(solution)/shard_map/ppermute | solution.py:407
  143.8 22.9 %all-to-all-start.2 = ((bf16[16,64,512]{2,1,0:T(8,128)(2,1)}), bf16[16,64,512]{2,1,0:T(8,128)(2,1)S(1)}, u32[]{:S(2)}, u32[]{:S(2)}) async-start(bf16[16,64,512]{2,1,0:T(8,128)(2,1)} %bitcast.20), calls=%async_computation.2 | async-start | bytes 2097152 | tf_op jit(solution)/shard_map/all_to_all | solution.py:368
  166.7 2.2 %copy-start.1 = (bf16[4096,512]{1,0:T(8,128)(2,1)S(1)}, bf16[4096,512]{1,0:T(8,128)(2,1)}, u32[]{:S(2)}) copy-start(bf16[4096,512]{1,0:T(8,128)(2,1)} %panel.3) | copy-start | bytes 12582916
  168.9 1.5 copy-start.3

commit v2 on v1

v2 whole, which is shorter than its diff:
```python
import functools

import jax
import jax.numpy as jnp
import numpy as np
from jax import lax
from jax.experimental import pallas as pl
from jax.experimental.pallas import tpu as pltpu
from jax.sharding import Mesh, PartitionSpec as P

NEG_WEIGHT = 0.0625
LEARN_RATE = 0.25

D = 512
BLOCK = 128
HOT = 1024
LHOT = 256
CAP = 64
VS = 256
CR = 512
NX = 4
NCORE = 2
NCOL = 16
NBLK = 128
SLOTS = LHOT + NCOL * CAP
HALF_SLOTS = SLOTS // 2
CHUNK = 16
STEPS = NBLK // CHUNK
BASE = 4096.0

F32 = jnp.float32
BF16 = jnp.bfloat16
I16 = jnp.int16
F8 = jnp.float8_e5m2
NN = (((1,), (0,)), ((), ()))
NT = (((1,), (1,)), ((), ()))
TN = (((0,), (0,)), ((), ()))


def dot(a, b, dims):
    return lax.dot_general(a, b, dims, preferred_element_type=F32)


def params(mib):
    return pltpu.CompilerParams(vmem_limit_bytes=mib * 2**20)


def cost(flops, nbytes):
    return pl.CostEstimate(flops=flops, bytes_accessed=nbytes, transcendentals=0)


def one_hot(rows, ids, weight=None):
    shape = (rows, ids.shape[1])
    index = lax.broadcasted_iota(jnp.int32, shape, 0).astype(I16)
    hit = index == jnp.broadcast_to(ids.astype(I16), shape)
    value = jnp.ones((), BF16) if weight is None else jnp.broadcast_to(weight, shape)
    return jnp.where(hit, value, jnp.zeros((), BF16))


def split(x):
    high = x.astype(BF16)
    return high, (x - high.astype(F32)).astype(BF16)


def count_step(first_row, pairs, codes, rows, left, right):
    width = right.shape[0]
    for n in range(CHUNK):
        at = slice(n * BLOCK, (n + 1) * BLOCK)
        code = codes[n : n + 1, :]
        upper = code >= HALF_SLOTS
        weight = jnp.where(upper, BASE, 1.0).astype(BF16)
        left[:, at] = one_hot(HALF_SLOTS, jnp.where(upper, code - HALF_SLOTS, code), weight)
        right[:, at] = one_hot(width, rows[n : n + 1, :] - first_row)
    packed = dot(left[...], right[...], NT)
    high = jnp.floor(packed * (1.0 / BASE))
    pairs[0:HALF_SLOTS] += packed - high * BASE
    pairs[HALF_SLOTS:SLOTS] += high


def tile_step(episode, step, tiles, tile_counts, codes, left, right):
    for n in range(CHUNK):
        at = slice(n * BLOCK, (n + 1) * BLOCK)
        code = codes[n : n + 1, :]
        tile = tiles[0, 0, episode, step * CHUNK + n]
        left[:, at] = one_hot(64, code >> 5).astype(F8)
        right[:, at] = one_hot(128, (code & 31) * 4 + tile).astype(F8)
    tile_counts[...] += dot(left[...], right[...], NT)


def first_count_kernel(codes, rows, pairs, left, right):
    @pl.when(pl.program_id(0) == 0)
    def _():
        pairs[...] = jnp.zeros_like(pairs)

    count_step(0, pairs, codes, rows, left, right)


def second_count_kernel(
    tiles, codes0, rows0, codes1, rows1, pairs0, tile_counts, pairs1,
    left0, right0, left1, right1, left2, right2,
):
    step = pl.program_id(0)

    @pl.when(step == 0)
    def _():
        pairs0[...] = jnp.zeros_like(pairs0)
        pairs1[...] = jnp.zeros_like(pairs1)
        tile_counts[...] = jnp.zeros_like(tile_counts)

    count_step(CR // 2, pairs0, codes0, rows0, left0, right0)
    count_step(0, pairs1, codes1, rows1, left1, right1)
    tile_step(0, step, tiles, tile_counts, codes0, left2, right2)


def count_scratch():
    edges = CHUNK * BLOCK
    return [pltpu.VMEM((HALF_SLOTS, edges), BF16), pltpu.VMEM((CR // 2, edges), BF16)]


def tile_scratch():
    edges = CHUNK * BLOCK
    return [pltpu.VMEM((64, edges), F8), pltpu.VMEM((128, edges), F8)]


SMEM = pl.BlockSpec(memory_space=pltpu.SMEM)


def whole(*shape):
    return pl.BlockSpec(shape, lambda i: (0,) * len(shape))


def edge_block(episode):
    return pl.BlockSpec(
        (None, None, None, CHUNK, BLOCK),
        lambda i: (0, 0, episode, jnp.minimum(i, STEPS - 1), 0),
    )


def first_counts(src_code, ctx_rows):
    return pl.pallas_call(
        first_count_kernel,
        out_shape=jax.ShapeDtypeStruct((SLOTS, CR // 2), F32),
        grid=(STEPS,),
        in_specs=[edge_block(0), edge_block(0)],
        out_specs=whole(SLOTS, CR // 2),
        scratch_shapes=count_scratch(),
        compiler_params=params(56),
        cost_estimate=cost(NBLK * BLOCK * HALF_SLOTS * CR, 3 << 20),
        name="first_counts",
    )(src_code, ctx_rows)


def second_counts(neg_tiles, src_code, ctx_rows):
    part = jax.ShapeDtypeStruct((SLOTS, CR // 2), F32)
    return pl.pallas_call(
        second_count_kernel,
        out_shape=[part, jax.ShapeDtypeStruct((64, 128), F32), part],
        grid=(STEPS,),
        in_specs=[SMEM, edge_block(0), edge_block(0), edge_block(1), edge_block(1)],
        out_specs=[whole(SLOTS, CR // 2), whole(64, 128), whole(SLOTS, CR // 2)],
        scratch_shapes=count_scratch() + count_scratch() + tile_scratch(),
        compiler_params=params(56),
        cost_estimate=cost(2 * NBLK * BLOCK * HALF_SLOTS * CR, 6 << 20),
        name="second_counts",
    )(neg_tiles, src_code, ctx_rows, src_code, ctx_rows)


def live_ids(ids, count):
    lane = lax.broadcasted_iota(jnp.int32, ids.shape, 1)
    return jnp.where(lane < count, ids, -1)


def pick_kernel(matching, pieces, out):
    for episode in range(2):
        for reader in range(NCOL):
            partner = matching[episode, reader]
            out[reader, episode] = pieces[partner]


def pick_pieces(matching, pieces):
    rows = pieces.shape[1]
    return pl.pallas_call(
        pick_kernel,
        out_shape=jax.ShapeDtypeStruct((NCOL, 2, rows, D), BF16),
        in_specs=[
            pl.BlockSpec(memory_space=pltpu.SMEM),
            pl.BlockSpec(memory_space=pltpu.VMEM),
        ],
        out_specs=pl.BlockSpec(memory_space=pltpu.VMEM),
        compiler_params=params(16),
        cost_estimate=cost(0, 2 << 20),
        name="pick_pieces",
    )(matching, pieces)


def main_kernel(
    tiles, cold_count, codes, rows, panel, hot_table, hot_list, cold_list, ctx,
    pairs0_low, pairs0_high, counts0, pairs1_low, cold, keep, send,
    left, right, left2, right2, pairs1_high, counts1, all_slots, all_grads, ctx_acc, hot_acc,
):
    step = pl.program_id(0)
    col = lax.axis_index("col")

    @pl.when(step == 0)
    def _():
        pairs1_high[...] = jnp.zeros_like(pairs1_high)
        counts1[...] = jnp.zeros_like(counts1)
        all_slots[0:LHOT] = dot(one_hot(HOT, hot_list[...]), hot_table[...], TN).astype(BF16)

    @pl.when(step < STEPS)
    def _():
        for o in range(2):
            owner = 2 * step + o
            ids = live_ids(cold_list[0, col, pl.ds(owner, 1), :], cold_count[0, col, owner])
            taken = dot(one_hot(VS, ids), panel[o * VS : (o + 1) * VS, :], TN)
            at = pl.multiple_of(LHOT + owner * CAP, CAP)
            all_slots[pl.ds(at, CAP)] = taken.astype(BF16)
        count_step(CR // 2, pairs1_high, codes, rows, left, right)
        tile_step(1, step, tiles, counts1, codes, left2, right2)

    @pl.when(step >= STEPS)
    def _():
        grad_step(
            step - STEPS, hot_list, ctx, pairs0_low, pairs0_high, counts0, pairs1_low, cold, keep,
            send, pairs1_high, counts1, all_slots, all_grads, ctx_acc, hot_acc,
        )


def grad_step(
    step, hot_list, ctx, pairs0_low, pairs0_high, counts0, pairs1_low, cold, keep, send,
    pairs1_high, counts1, all_slots, all_grads, ctx_acc, hot_acc,
):
    slot_rows = pl.ds(pl.multiple_of(step * LHOT, LHOT), LHOT)
    here = all_slots[slot_rows]
    slot_at = step * LHOT + lax.broadcasted_iota(jnp.int32, (LHOT, 64), 0)
    group = ((slot_at >> 5) == lax.broadcasted_iota(jnp.int32, (LHOT, 64), 1)).astype(F32).astype(BF16)
    lane = lax.broadcasted_iota(jnp.int32, (LHOT, 256), 1)
    slot_in = lax.broadcasted_iota(jnp.int32, (LHOT, 256), 0) & 31
    mine = ((lane & 127) >> 2) == slot_in
    pick_row = lax.broadcasted_iota(jnp.int32, (256, CR), 0)
    pick_col = lax.broadcasted_iota(jnp.int32, (256, CR), 1)
    spread = jnp.where(
        (pick_row & 3) == (pick_col >> 7), jnp.where(pick_row >= 128, 128.0, 1.0), 0.0
    ).astype(BF16)
    total = None
    grads = []
    for episode in range(2):
        panel = ctx[:, episode].reshape(CR, D)
        if episode == 0:
            counted = jnp.concatenate([pairs0_low[...], pairs0_high[...]], 1)
        else:
            counted = jnp.concatenate([pairs1_low[...], pairs1_high[slot_rows]], 1)
        table = (counts0, counts1)[episode][...]
        upper = jnp.floor(table * (1.0 / 128.0))
        both = jnp.concatenate([table - upper * 128.0, upper], 1).astype(BF16)
        taken = jnp.where(mine, dot(group, both, NN), 0.0).astype(BF16)
        tiled = dot(taken, spread, NN)
        curve = jnp.tanh(0.5 * dot(here, panel, NT))
        negative = (0.5 * NEG_WEIGHT + (0.5 * NEG_WEIGHT) * curve).astype(BF16).astype(F32)
        grad = tiled * negative - counted * (0.5 - 0.5 * curve)
        high = grad.astype(BF16)
        grads.append((grad, high, panel))
        part = dot(high, panel, NN)
        total = part if total is None else total + part
        all_grads[episode, slot_rows] = high

    @pl.when(step == 0)
    def _():
        full = total
        for grad, high, panel in grads:
            full = full + dot((grad - high.astype(F32)).astype(BF16), panel, NN)
        upper, lower = split(full)
        where_hot = one_hot(HOT, hot_list[...])
        hot_acc[...] = dot(where_hot, upper, NN) + dot(where_hot, lower, NN)

    @pl.when(step > 0)
    def _():
        for o in range(4):
            cold[o] = total[o * CAP : (o + 1) * CAP].astype(BF16)

    @pl.when(step == 4)
    def _():
        for episode in range(2):
            ctx_acc[episode] = dot(all_grads[episode], all_slots[...], TN)
        core = lax.axis_index("core")
        for half, out in ((core, keep), (1 - core, send)):
            for away in range(NX):
                x = lax.axis_index("x") ^ away
                hot_at = pl.multiple_of(half * (HOT // 2) + x * 128, 128)
                ctx_at = pl.multiple_of(half * (CR // 2) + x * 64, 64)
                out[away, 0:128] = hot_acc[pl.ds(hot_at, 128)].astype(out.dtype)
                out[away, 128:192] = ctx_acc[0, pl.ds(ctx_at, 64)].astype(out.dtype)
                out[away, 192:256] = ctx_acc[1, pl.ds(ctx_at, 64)].astype(out.dtype)


def gradients(
    neg_tiles, cold_count, src_code, ctx_rows, panel, hot_table, hot_list, cold_list, ctx, counts
):
    later = lambda i: jnp.maximum(i - STEPS, 0)
    half = pl.BlockSpec((LHOT, CR // 2), lambda i: (later(i), 0))
    part = lambda dtype: jax.ShapeDtypeStruct((NX, 256, D), dtype)
    return pl.pallas_call(
        main_kernel,
        out_shape=[jax.ShapeDtypeStruct((NCOL, CAP, D), BF16), part(F32), part(BF16)],
        grid=(STEPS + 5,),
        in_specs=[
            SMEM,
            SMEM,
            edge_block(1),
            edge_block(1),
            pl.BlockSpec((2 * VS, D), lambda i: (jnp.minimum(i, STEPS - 1), 0)),
            whole(HOT, D),
            whole(1, LHOT),
            whole(1, NCOL, NCOL, CAP),
            whole(NCOL, 2, CR // NCOL, D),
            half,
            half,
            whole(64, 128),
            half,
        ],
        out_specs=[
            pl.BlockSpec((4, CAP, D), lambda i: (later(i - 1), 0, 0)),
            whole(NX, 256, D),
            whole(NX, 256, D),
        ],
        scratch_shapes=count_scratch()
        + tile_scratch()
        + [
            pltpu.VMEM((SLOTS, CR // 2), F32),
            pltpu.VMEM((64, 128), F32),
            pltpu.VMEM((SLOTS, D), BF16),
            pltpu.VMEM((2, SLOTS, CR), BF16),
            pltpu.VMEM((2, CR, D), F32),
            pltpu.VMEM((HOT, D), F32),
        ],
        compiler_params=params(56),
        cost_estimate=cost(28 << 30, 12 << 20),
        name="gradients",
    )(
        neg_tiles, cold_count, src_code, ctx_rows, panel, hot_table, hot_list, cold_list, ctx,
        *counts,
    )


def x_sum_kernel(own, first, second, third, out):
    total = own[...]
    for part in (first, second, third):
        total += part[...].astype(F32)
    for j in range(NCOL):
        pair = jnp.concatenate([total[j * 8 : j * 8 + 8], total[128 + j * 8 : 136 + j * 8]], 0)
        out[j] = pair.astype(BF16)


def x_sum(own, others):
    return pl.pallas_call(
        x_sum_kernel,
        out_shape=jax.ShapeDtypeStruct((NCOL, 16, D), BF16),
        compiler_params=params(16),
        cost_estimate=cost(1 << 20, 2 << 20),
        name="x_sum",
    )(own, *others)


def col_sum_kernel(matching, parts, out):
    episode = lax.axis_index("col") // (NCOL // 2)
    hot = parts[0].astype(F32)[0:8]
    for c in range(1, NCOL):
        hot += parts[c].astype(F32)[0:8]
    for q in range(NCOL):
        step = parts[matching[episode, q]].astype(F32)[8:16]
        pair = jnp.concatenate([hot, step], 0).astype(BF16)
        for x in range(NX):
            out[x, q] = pair


def col_sum(matching, parts):
    return pl.pallas_call(
        col_sum_kernel,
        out_shape=jax.ShapeDtypeStruct((NX, NCOL, 16, D), BF16),
        in_specs=[SMEM, pl.BlockSpec(memory_space=pltpu.VMEM)],
        out_specs=pl.BlockSpec(memory_space=pltpu.VMEM),
        compiler_params=params(16),
        cost_estimate=cost(1 << 20, 2 << 20),
        name="col_sum",
    )(matching, parts)


def finish_kernel(own, other, hot_table, context, hot_out, context_out):
    for from_other, parts in ((0, own), (1, other)):
        half = lax.axis_index("core") ^ from_other
        for x in range(NX):
            hot_at = pl.multiple_of(half * (HOT // 2) + x * 128, 128)
            ctx_at = pl.multiple_of(half * (CR // 2) + x * 64, 64)
            first = [parts[x, j].astype(F32) for j in range(NCOL)]
            hot = jnp.concatenate([p[0:8] for p in first], 0)
            step = jnp.concatenate([first[j][8:16] + first[j + 8][8:16] for j in range(8)], 0)
            hot_rows = hot_table[pl.ds(hot_at, 128)].astype(F32)
            hot_out[pl.ds(hot_at, 128)] = hot_rows - LEARN_RATE * hot
            ctx_rows = context[pl.ds(ctx_at, 64)].astype(F32)
            context_out[pl.ds(ctx_at, 64)] = ctx_rows - LEARN_RATE * step


def finish(own, other, hot_table, context):
    vmem = pl.BlockSpec(memory_space=pltpu.VMEM)
    return pl.pallas_call(
        finish_kernel,
        out_shape=[jax.ShapeDtypeStruct((HOT, D), F32), jax.ShapeDtypeStruct((CR, D), F32)],
        in_specs=[vmem, vmem, vmem, vmem],
        out_specs=[vmem, vmem],
        compiler_params=params(24),
        cost_estimate=cost(1 << 20, 7 << 20),
        name="finish",
    )(own, other, hot_table, context)


def vertex_kernel(col, cold_count, cold_list, received, panel, out):
    total = jnp.zeros((VS, D), F32)
    for c in range(NCOL):
        ids = live_ids(cold_list[0, c, pl.ds(col[0], 1), :], cold_count[0, c, col[0]])
        total += dot(one_hot(VS, ids), received[c], NN)
    out[...] = panel[...].astype(F32) - LEARN_RATE * total


def vertex_rows(col, cold_count, cold_list, received, panel):
    keep = lambda *shape: pl.BlockSpec(shape, lambda i, c: (0,) * len(shape))
    return pl.pallas_call(
        vertex_kernel,
        out_shape=jax.ShapeDtypeStruct((VS, D), F32),
        grid_spec=pltpu.PrefetchScalarGridSpec(
            num_scalar_prefetch=1,
            grid=(1,),
            in_specs=[
                SMEM,
                keep(1, NCOL, NCOL, CAP),
                keep(NCOL, CAP, D),
                pl.BlockSpec((VS, D), lambda i, c: (c[0], 0)),
            ],
            out_specs=keep(VS, D),
        ),
        compiler_params=params(56),
        cost_estimate=cost(1 << 28, 2 << 20),
        name="vertex_rows",
    )(col, cold_count, cold_list, received, panel)


def all_to_all(x, axes):
    return lax.all_to_all(x, axes, 0, 0, tiled=True)


def body(
    vertex_panel,
    context_panel,
    hot_table,
    matching,
    hot_map,
    cold_list,
    cold_count,
    src_code,
    ctx_rows,
    neg_tiles,
):
    col = lax.axis_index("col").astype(jnp.int32)[None]
    swap = [(0, 1), (1, 0)]

    pieces = all_to_all(context_panel.reshape(NCOL, CR // NCOL, D), "col")
    low = first_counts(src_code, ctx_rows)
    low, pieces = lax.optimization_barrier((low, pieces))
    ctx = all_to_all(pick_pieces(matching, pieces), "col")
    counts = (low, *second_counts(neg_tiles, src_code, ctx_rows))

    cold, keep, send = gradients(
        neg_tiles, cold_count, src_code, ctx_rows, vertex_panel, hot_table, hot_map[0],
        cold_list, ctx, counts,
    )
    received = all_to_all(cold, "col")
    arrived = lax.ppermute(send, "core", swap)
    parts = keep + arrived.astype(F32)
    others = [
        lax.ppermute(parts[k].astype(BF16), "x", [(i, i ^ k) for i in range(NX)])
        for k in range(1, NX)
    ]
    parts = x_sum(parts[0], others)
    received, parts = lax.optimization_barrier((received, parts))
    parts = all_to_all(parts, "col")
    parts = col_sum(matching, parts).reshape(NX * NCOL, 16, D)
    own = all_to_all(parts, ("x", "col")).reshape(NX, NCOL, 16, D)
    other = lax.ppermute(own, "core", swap)
    vertex_new = vertex_rows(col, cold_count, cold_list, received, vertex_panel)
    hot_new, context_new = finish(own, other, hot_table, context_panel)
    return (vertex_new, context_new, hot_new)


def solution(mesh):
    split_mesh = Mesh(mesh.devices.reshape(NX, NCORE, NCOL), ("x", "core", "col"))
    row = ("x", "core")
    in_specs = (
        P(row, None),
        P("col", None),
        P(),
        P(),
        P(row, "col", None),
        P(row, None, None, None),
        P(row, None, None),
        P(row, "col", None, None, None),
        P(row, "col", None, None, None),
        P(row, "col", None, None),
    )
    out_specs = (P(("x", "core", "col"), None), P("col", None), P())
    return jax.shard_map(
        body, mesh=split_mesh, in_specs=in_specs, out_specs=out_specs, check_vma=False
    )
```

time: 174 us -> 145 us (0.83)
  waiting for transfers between devices: 30.6 us -> 13.7 us
  local copies, waits for them, and re-layouts: 10.1 us -> 1.08 us
  blocking collectives: 38.1 us -> 32.5 us
    all_to_all x4 -> x3, waiting for transfers between devices: 26.6 us -> 0.32 us  [all_to_all(): return lax.all_to_all(x, axes, 0, 0, tiled=True)]
    ppermute x2 -> x5, waiting for transfers between devices: 4 us -> 13.4 us  [the longest x3 13.4 us: body(): lax.ppermute(parts[k].astype(BF16), 'x', [(i, i ^ k) for i in range(NX)])]
    unnamed x34 -> x12, local copies, waits for them, and re-layouts: 9.94 us -> 0.99 us
    all_to_all x2, blocking collectives: 38.1 us -> 32.5 us  [all_to_all(): return lax.all_to_all(x, axes, 0, 0, tiled=True)]
    ppermute x2 -> x5, starting transfers between devices: 5.38 us -> 10.1 us  [the longest x1 4.57 us: body(): other = lax.ppermute(own, 'core', swap)]
    all_to_all x4 -> x3, starting transfers between devices: 25.8 us -> 21.9 us  [all_to_all(): return lax.all_to_all(x, axes, 0, 0, tiled=True)]
    pallas_call x1, Pallas kernels: 1.48 us -> 3.44 us  [vertex_rows(): pl.pallas_call(vertex_kernel, out_shape=jax.ShapeDtypeStruct((VS, D), F32...]
    pallas_call x4 -> x3, Pallas kernels: 54.2 us -> 54.3 us  [the longest x1 24.7 us: gradients(): pl.pallas_call(main_kernel, out_shape=[jax.ShapeDtypeStruct((NCOL, CAP, D...]
  transfers between devices with their start and end apart: 6 -> 8, of which waited for: 3 -> 4; matrix products, arithmetic and copies ran while one was open for 0% -> 1% of each run, Pallas kernels for 23% -> 23%
where the time goes in v2:
time: 145 us; the launch traced here: 144 us
  Pallas kernels  62.2 us (43%)
  blocking collectives  32.5 us (22%)
  starting transfers between devices  32 us (22%)
  waiting for transfers between devices  13.7 us (9%)
  other arithmetic  1.68 us (1%)
    all_to_all x2, blocking collectives, all_to_all(): return lax.all_to_all(x, axes, 0, 0, tiled=True)  32.5 us
    pallas_call x1, Pallas kernels, gradients(): pl.pallas_call(main_kernel, out_shape=[jax.ShapeDtypeStruct((NCOL, CAP, D...  24.7 us
    all_to_all x3, starting transfers between devices, all_to_all(): return lax.all_to_all(x, axes, 0, 0, tiled=True)  21.9 us
    pallas_call x1, Pallas kernels, second_counts(): pl.pallas_call(second_count_kernel, out_shape=[part, jax.ShapeDtypeStruct...  19.4 us
    ppermute x3, waiting for transfers between devices, body(): lax.ppermute(parts[k].astype(BF16), 'x', [(i, i ^ k) for i in range(NX)])  13.4 us
    pallas_call x1, Pallas kernels, first_counts(): pl.pallas_call(first_count_kernel, out_shape=jax.ShapeDtypeStruct((SLOTS,...  10.2 us
    ppermute x1, starting transfers between devices, body(): other = lax.ppermute(own, 'core', swap)  4.57 us
    ppermute x3, starting transfers between devices, body(): lax.ppermute(parts[k].astype(BF16), 'x', [(i, i ^ k) for i in range(NX)])  3.94 us
  transfers between devices with their start and end apart: 8, of which 4 were waited for; matrix products, arithmetic and copies ran while one was open for 1% of the time, Pallas kernels for 23%

profile of v2, /device:TPU:1, one launch (start us, length us, event | category | flops | bytes accessed | tf_op | source)
XLA Modules:
  0.0 143.9 jit_solution(8860734916606447488)
XLA Ops:
  0.6 8.6 %all-to-all-start = ((bf16[16,32,512]{2,1,0:T(8,128)(2,1)}), bf16[16,32,512]{2,1,0:T(8,128)(2,1)S(1)}, u32[]{:S(2)}, u32[]{:S(2)}) async-start(bf16[16,32,512]{2,1,0:T(8,128)(2,1)} %bitcast.16), calls=%async_computation | async-start | bytes 1048576 | tf_op jit(solution)/shard_map/all_to_all | solution.py:447
  9.2 0.0 copy-start.2
  9.3 10.2 %first_counts.1.pairs0_low = f32[1280,256]{1,0:T(8,128)} custom-call(s32[1,1,2,128,128]{4,3,2,1,0:T(8,128)} %codes.3, s32[1,1,2,128,128]{4,3,2,1,0:T(8,128)} %rows.3), custom_call_target="tpu_custom_call" | custom-call | flops 5368709120 | bytes 3145728 | tf_op jit(solution)/shard_map/first_counts/pallas_call | solution.py:140
  19.4 0.3 all-to-all-done.pieces
  19.8 1.6 %pick_pieces.1 = bf16[16,2,32,512]{3,2,1,0:T(8,128)(2,1)} custom-call(s32[2,16]{1,0:T(2,128)S(1)} %copy-done.2, bf16[16,32,512]{2,1,0:T(8,128)(2,1)S(1)} %all-to-all-done.pieces), custom_call_target="tpu_custom_call" | custom-call | bytes 2097152 | tf_op jit(solution)/shard_map/pick_pieces/pallas_call | solution.py:182
  21.4 6.3 %all-to-all-start.1 = ((bf16[16,2,32,512]{3,2,1,0:T(8,128)(2,1)}), bf16[16,2,32,512]{3,2,1,0:T(8,128)(2,1)S(1)}, u32[]{:S(2)}, u32[]{:S(2)}) async-start(bf16[16,2,32,512]{3,2,1,0:T(8,128)(2,1)} %pick_pieces.1), calls=%async_computation.1 | async-start | bytes 2097152 | tf_op jit(solution)/shard_map/all_to_all | solution.py:447
  27.7 19.4 %second_counts.1 = (f32[1280,256]{1,0:T(8,128)}, f32[64,128]{1,0:T(8,128)}, f32[1280,256]{1,0:T(8,128)}) custom-call(s32[1,1,2,128]{3,2,1,0:T(2,128)} %tiles.3, s32[1,1,2,128,128]{4,3,2,1,0:T(8,128)} %codes.3, s32[1,1,2,128,128]{4,3,2,1,0:T(8,128)} %rows.3, s32[1,1,2,128,128]{4,3,2,1,0:T(8,128)} %codes.3, s32[1,1,2,128,128]{4,3,2,1,0:T(8,128)} %rows.3), custom_call_target="tpu_custom_call" | custom-call | flops 10737418240 | bytes 6291456 | tf_op jit(solution)/shard_map/second_counts/pallas_call | solution.py:155
  47.1 0.0 all-to-all-done.1.ctx
  47.1 1.0 copy-done.5
  48.1 24.7 %gradients.1 = (bf16[16,64,512]{2,1,0:T(8,128)(2,1)}, f32[4,256,512]{2,1,0:T(8,128)}, bf16[4,256,512]{2,1,0:T(8,128)(2,1)}) custom-call(s32[1,1,2,128]{3,2,1,0:T(2,128)} %tiles.3, s32[1,16,16]{2,1,0:T(8,128)} %cold_count.3, s32[1,1,2,128,128]{4,3,2,1,0:T(8,128)} %codes.3, s32[1,1,2,128,128]{4,3,2,1,0:T(8,128)} %rows.3, bf16[4096,512]{1,0:T(8,128)(2,1)} %panel.3, ...), custom_call_target="tpu_custom_call" | custom-call | flops 30064771072 | bytes 12582912 | tf_op jit(solution)/shard_map/gradients/pallas_call | solution.py:302
  72.8 0.0 copy-start.4
  72.8 1.6 %collective-permute-start = (bf16[4,256,512]{2,1,0:T(8,128)(2,1)}, bf16[4,256,512]{2,1,0:T(8,128)(2,1)}, u32[]{:S(2)}, u32[]{:S(2)}) collective-permute-start(bf16[4,256,512]{2,1,0:T(8,128)(2,1)} %get-tuple-element.22), channel_id=1, source_target_pairs={{0,16},{16,0},{1,17},{17,1},{2,18},{18,2},{3,19},{19,3},{4,20},{20... | collective-permute-start | bytes 3145736 | tf_op jit(solution)/shard_map/ppermute | solution.py:476
  74.4 6.9 %all-to-all-start.2 = ((bf16[16,64,512]{2,1,0:T(8,128)(2,1)}), bf16[16,64,512]{2,1,0:T(8,128)(2,1)S(1)}, u32[]{:S(2)}, u32[]{:S(2)}) async-start(bf16[16,64,512]{2,1,0:T(8,128)(2,1)} %get-tuple-element.20), calls=%async_computation.2 | async-start | bytes 2097152 | tf_op jit(solution)/shard_map/all_to_all | solution.py:447
  81.4 0.0 collective-permute-done
  81.4 1.7 %fusion = (bf16[4,256,512]{2,1,0:T(8,128)(2,1)S(1)}, f32[4,256,512]{2,1,0:T(8,128)S(1)}) fusion(f32[4,256,512]{2,1,0:T(8,128)S(1)} %copy-done.4, bf16[4,256,512]{2,1,0:T(8,128)(2,1)} %collective-permute-done), kind=kLoop, calls=%fused_computation.5 | loop fusion | flops 1572864 | bytes 6291456 | tf_op jit(solution)/shard_map/convert.2
  83.1 0.1 slice_bitcast_fusion.1
  83.1 1.3 collective-permute-start.1
  84.4 2.4 %collective-permute-start.2 = (bf16[256,512]{1,0:T(8,128)(2,1)S(1)}, bf16[256,512]{1,0:T(8,128)(2,1)S(1)}, u32[]{:S(2)}, u32[]{:S(2)}) collective-permute-start(bf16[256,512]{1,0:T(8,128)(2,1)S(1)} %get-tuple-element.30), channel_id=1, source_target_pairs={{0,64},{32,96},{64,0},{96,32},{1,65},{33,97},{65,1},{97,33},{2,66}... | collective-permute-start | bytes 786440 | tf_op jit(solution)/shard_map/ppermute | solution.py:479
  86.9 0.2 collective-permute-start.3
  87.1 3.5 %collective-permute-done.1.first = bf16[256,512]{1,0:T(8,128)(2,1)S(1)} collective-permute-done((bf16[256,512]{1,0:T(8,128)(2,1)S(1)}, bf16[256,512]{1,0:T(8,128)(2,1)S(1)}, u32[]{:S(2)}, u32[]{:S(2)}) %collective-permute-start.1) | collective-permute-done | bytes 262176 | tf_op jit(solution)/shard_map/ppermute | solution.py:479
  90.6 7.9 %collective-permute-done.2.second = bf16[256,512]{1,0:T(8,128)(2,1)S(1)} collective-permute-done((bf16[256,512]{1,0:T(8,128)(2,1)S(1)}, bf16[256,512]{1,0:T(8,128)(2,1)S(1)}, u32[]{:S(2)}, u32[]{:S(2)}) %collective-permute-start.2) | collective-permute-done | bytes 262176 | tf_op jit(solution)/shard_map/ppermute | solution.py:479
  98.5 2.0 %collective-permute-done.3.third = bf16[256,512]{1,0:T(8,128)(2,1)S(1)} collective-permute-done((bf16[256,512]{1,0:T(8,128)(2,1)S(1)}, bf16[256,512]{1,0:T(8,128)(2,1)S(1)}, u32[]{:S(2)}, u32[]{:S(2)}) %collective-permute-start.3) | collective-permute-done | bytes 262176 | tf_op jit(solution)/shard_map/ppermute | solution.py:479
  100.5 0.1 x_sum.1
  100.6 0.0 all-to-all-done.2.received
  100.6 0.0 copy-start.3
  100.6 13.7 %all_to_all.25.parts = bf16[16,16,512]{2,1,0:T(8,128)(2,1)S(1)} all-to-all(bf16[16,16,512]{2,1,0:T(8,128)(2,1)S(1)} %x_sum.1), channel_id=1, replica_groups=mesh['x'=4,'core'=2,'col'=16] {'col'}, dimensions={0} | all-to-all | bytes 524288 | tf_op jit(solution)/shard_map/all_to_all | solution.py:447
  114.4 0.7 col_sum.1
  115.0 18.8 %all_to_all.26 = bf16[64,16,512]{2,1,0:T(8,128)(2,1)S(1)} all-to-all(bf16[64,16,512]{2,1,0:T(8,128)(2,1)S(1)} %bitcast.15), channel_id=1, replica_groups=mesh['x'=4,'core'=2,'col'=16] {'x','col'}, dimensions={0} | all-to-all | bytes 2097152 | tf_op jit(solution)/shard_map/all_to_all | solution.py:447
  133.8 4.6 %collective-permute-start.4 = (bf16[4,16,16,512]{3,2,1,0:T(8,128)(2,1)S(1)}, bf16[4,16,16,512]{3,2,1,0:T(8,128)(2,1)S(1)}, u32[]{:S(2)}, u32[]{:S(2)}) collective-permute-start(bf16[4,16,16,512]{3,2,1,0:T(8,128)(2,1)S(1)} %bitcast.13), channel_id=1, source_target_pairs={{0,16},{16,0},{1,17},{17,1},{2,18},{18,2},{3,19},{19,3},{4,20},{20... | collective-permute-start | bytes 3145736 | tf_op jit(solution)/shard_map/ppermute | solution.py:487
  138.4 3.4 %vertex_rows.1 = f32[256,512]{1,0:T(8,128)} custom-call(s32[1]{0:T(128)} %bitcast.col, s32[1,16,16]{2,1,0:T(8,128)} %cold_count.3, s32[1,16,16,64]{3,2,1,0:T(8,128)} %cold_list.3, bf16[16,64,512]{2,1,0:T(8,128)(2,1)} %copy-done.3, bf16[4096,512]{1,0:T(8,128)(2,1)} %panel.3), custom_call_target="tpu_custom_call" | custom-call | flops 268435456 | bytes 2097152 | tf_op jit(solution)/shard_map/vertex_rows/pallas_call | solution.py:426
  141.8 0.0 collective-permute-done.4.other
  141.8 2.1 %finish.1 = (f32[1024,512]{1,0:T(8,128)}, f32[512,512]{1,0:T(8,128)}) custom-call(bf16[4,16,16,512]{3,2,1,0:T(8,128)(2,1)S(1)} %bitcast.14, bf16[4,16,16,512]{3,2,1,0:T(8,128)(2,1)S(1)} %collective-permute-done.4.other, bf16[1024,512]{1,0:T(8,128)(2,1)S(1)} %copy-done.1, bf16[512,512]{1,0:T(8,128)(2,1)S(1)} %copy-done), custom_call_target="tpu_custom_call" | custom-call | flops 1048576 | bytes 7340032 | tf_op jit(solution)/shard_map/finish/pallas_call | solution.py:405
  (9 shorter events, 0.1 us)
Async XLA Ops:
  0.6 19.1 %all-to-all-start = ((bf16[16,32,512]{2,1,0:T(8,128)(2,1)}), bf16[16,32,512]{2,1,0:T(8,128)(2,1)S(1)}, u32[]{:S(2)}, u32[]{:S(2)}) async-start(bf16[16,32,512]{2,1,0:T(8,128)(2,1)} %bitcast.16), calls=%async_computation | async-start | bytes 1048576 | tf_op jit(solution)/shard_map/all_to_all | solution.py:447
  9.2 10.5 %copy-start.2 = (s32[2,16]{1,0:T(2,128)S(1)}, s32[2,16]{1,0:T(2,128)}, u32[]{:S(2)}) copy-start(s32[2,16]{1,0:T(2,128)} %matching.3) | copy-start | bytes 388
  21.4 25.8 %all-to-all-start.1 = ((bf16[16,2,32,512]{3,2,1,0:T(8,128)(2,1)}), bf16[16,2,32,512]{3,2,1,0:T(8,128)(2,1)S(1)}, u32[]{:S(2)}, u32[]{:S(2)}) async-start(bf16[16,2,32,512]{3,2,1,0:T(8,128)(2,1)} %pick_pieces.1), calls=%async_computation.1 | async-start | bytes 2097152 | tf_op jit(solution)/shard_map/all_to_all | solution.py:447
  47.1 1.0 copy-start.5
  72.8 8.6 %copy-start.4 = (f32[4,256,512]{2,1,0:T(8,128)S(1)}, f32[4,256,512]{2,1,0:T(8,128)}, u32[]{:S(2)}) copy-start(f32[4,256,512]{2,1,0:T(8,128)} %get-tuple-element.21) | copy-start | bytes 6291460
  72.8 8.5 %collective-permute-start = (bf16[4,256,512]{2,1,0:T(8,128)(2,1)}, bf16[4,256,512]{2,1,0:T(8,128)(2,1)}, u32[]{:S(2)}, u32[]{:S(2)}) collective-permute-start(bf16[4,256,512]{2,1,0:T(8,128)(2,1)} %get-tuple-element.22), channel_id=1, source_target_pairs={{0,16},{16,0},{1,17},{17,1},{2,18},{18,2},{3,19},{19,3},{4,20},{20... | collective-permute-start | bytes 3145736 | tf_op jit(solution)/shard_map/ppermute | solution.py:476
  74.4 26.2 %all-to-all-start.2 = ((bf16[16,64,512]{2,1,0:T(8,128)(2,1)}), bf16[16,64,512]{2,1,0:T(8,128)(2,1)S(1)}, u32[]{:S(2)}, u32[]{:S(2)}) async-start(bf16[16,64,512]{2,1,0:T(8,128)(2,1)} %get-tuple-element.20), calls=%async_computation.2 | async-start | bytes 2097152 | tf_op jit(solution)/shard_map/all_to_all | solution.py:447
  83.1 7.5 %collective-permute-start.1 = (bf16[256,512]{1,0:T(8,128)(2,1)S(1)}, bf16[256,512]{1,0:T(8,128)(2,1)S(1)}, u32[]{:S(2)}, u32[]{:S(2)}) collective-permute-start(bf16[256,512]{1,0:T(8,128)(2,1)S(1)} %get-tuple-element.31), channel_id=1, source_target_pairs={{0,32},{32,0},{64,96},{96,64},{1,33},{33,1},{65,97},{97,65},{2,34}... | collective-permute-start | bytes 786440 | tf_op jit(solution)/shard_map/ppermute | solution.py:479
  84.4 14.1 %collective-permute-start.2 = (bf16[256,512]{1,0:T(8,128)(2,1)S(1)}, bf16[256,512]{1,0:T(8,128)(2,1)S(1)}, u32[]{:S(2)}, u32[]{:S(2)}) collective-permute-start(bf16[256,512]{1,0:T(8,128)(2,1)S(1)} %get-tuple-element.30), channel_id=1, source_target_pairs={{0,64},{32,96},{64,0},{96,32},{1,65},{33,97},{65,1},{97,33},{2,66}... | collective-permute-start | bytes 786440 | tf_op jit(solution)/shard_map/ppermute | solution.py:479
  86.9 13.6 %collective-permute-start.3 = (bf16[256,512]{1,0:T(8,128)(2,1)S(1)}, bf16[256,512]{1,0:T(8,128)(2,1)S(1)}, u32[]{:S(2)}, u32[]{:S(2)}) collective-permute-start(bf16[256,512]{1,0:T(8,128)(2,1)S(1)} %get-tuple-element.29), channel_id=1, source_target_pairs={{0,96},{32,64},{64,32},{96,0},{1,97},{33,65},{65,33},{97,1},{2,98}... | collective-permute-start | bytes 786440 | tf_op jit(solution)/shard_map/ppermute | solution.py:479
  100.6 37.7 %copy-start.3 = (bf16[16,64,512]{2,1,0:T(8,128)(2,1)}, bf16[16,64,512]{2,1,0:T(8,128)(2,1)S(1)}, u32[]{:S(2)}) copy-start(bf16[16,64,512]{2,1,0:T(8,128)(2,1)S(1)} %all-to-all-done.2.received) | copy-start | bytes 3145732
  133.8 8.0 %collective-permute-start.4 = (bf16[4,16,16,512]{3,2,1,0:T(8,128)(2,1)S(1)}, bf16[4,16,16,512]{3,2,1,0:T(8,128)(2,1)S(1)}, u32[]{:S(2)}, u32[]{:S(2)}) collective-permute-start(bf16[4,16,16,512]{3,2,1,0:T(8,128)(2,1)S(1)} %bitcast.13), channel_id=1, source_target_pairs={{0,16},{16,0},{1,17},{17,1},{2,18},{18,2},{3,19},{19,3},{4,20},{20... | collective-permute-start | bytes 3145736 | tf_op jit(solution)/shard_map/ppermute | solution.py:487
  138.3 3.5 %copy-start = (bf16[512,512]{1,0:T(8,128)(2,1)S(1)}, bf16[512,512]{1,0:T(8,128)(2,1)}, u32[]{:S(2)}) copy-start(bf16[512,512]{1,0:T(8,128)(2,1)} %context.1) | copy-start | bytes 1572868
  138.4 3.5 %copy-start.1 = (bf16[1024,512]{1,0:T(8,128)(2,1)S(1)}, bf16[1024,512]{1,0:T(8,128)(2,1)}, u32[]{:S(2)}) copy-start(bf16[1024,512]{1,0:T(8,128)(2,1)} %hot_table.3) | copy-start | bytes 3145732

commit v3 on v2

--- a/solution.py
+++ b/solution.py
@@ -96,7 +96,7 @@
 
 
 def second_count_kernel(
-    tiles, codes0, rows0, codes1, rows1, pairs0, tile_counts, pairs1,
+    tiles, codes0, rows0, codes1, rows1, pairs0, pairs1,
     left0, right0, left1, right1, left2, right2,
 ):
     step = pl.program_id(0)
@@ -105,11 +105,10 @@
     def _():
         pairs0[...] = jnp.zeros_like(pairs0)
         pairs1[...] = jnp.zeros_like(pairs1)
-        tile_counts[...] = jnp.zeros_like(tile_counts)
 
     count_step(CR // 2, pairs0, codes0, rows0, left0, right0)
     count_step(0, pairs1, codes1, rows1, left1, right1)
-    tile_step(0, step, tiles, tile_counts, codes0, left2, right2)
+    tile_step(0, step, tiles, pairs0.at[SLOTS : SLOTS + 64, 0:128], codes0, left2, right2)
 
 
 def count_scratch():
@@ -151,13 +150,13 @@
 
 
 def second_counts(neg_tiles, src_code, ctx_rows):
-    part = jax.ShapeDtypeStruct((SLOTS, CR // 2), F32)
+    shapes = [(SLOTS + 64, CR // 2), (SLOTS, CR // 2)]
     return pl.pallas_call(
         second_count_kernel,
-        out_shape=[part, jax.ShapeDtypeStruct((64, 128), F32), part],
+        out_shape=[jax.ShapeDtypeStruct(shape, F32) for shape in shapes],
         grid=(STEPS,),
         in_specs=[SMEM, edge_block(0), edge_block(0), edge_block(1), edge_block(1)],
-        out_specs=[whole(SLOTS, CR // 2), whole(64, 128), whole(SLOTS, CR // 2)],
+        out_specs=[whole(*shape) for shape in shapes],
         scratch_shapes=count_scratch() + count_scratch() + tile_scratch(),
         compiler_params=params(56),
         cost_estimate=cost(2 * NBLK * BLOCK * HALF_SLOTS * CR, 6 << 20),
@@ -237,10 +236,10 @@
     lane = lax.broadcasted_iota(jnp.int32, (LHOT, 256), 1)
     slot_in = lax.broadcasted_iota(jnp.int32, (LHOT, 256), 0) & 31
     mine = ((lane & 127) >> 2) == slot_in
-    pick_row = lax.broadcasted_iota(jnp.int32, (256, CR), 0)
-    pick_col = lax.broadcasted_iota(jnp.int32, (256, CR), 1)
+    pick_row = lax.broadcasted_iota(jnp.int32, (256, 128), 0)
+    pick_col = lax.broadcasted_iota(jnp.int32, (256, 128), 1)
     spread = jnp.where(
-        (pick_row & 3) == (pick_col >> 7), jnp.where(pick_row >= 128, 128.0, 1.0), 0.0
+        (pick_row & 3) == pick_col, jnp.where(pick_row >= 128, 128.0, 1.0), 0.0
     ).astype(BF16)
     total = None
     grads = []
@@ -254,7 +253,10 @@
         upper = jnp.floor(table * (1.0 / 128.0))
         both = jnp.concatenate([table - upper * 128.0, upper], 1).astype(BF16)
         taken = jnp.where(mine, dot(group, both, NN), 0.0).astype(BF16)
-        tiled = dot(taken, spread, NN)
+        by_tile = dot(taken, spread, NN)
+        tiled = jnp.concatenate(
+            [jnp.broadcast_to(by_tile[:, t : t + 1], (LHOT, BLOCK)) for t in range(4)], 1
+        )
         curve = jnp.tanh(0.5 * dot(here, panel, NT))
         negative = (0.5 * NEG_WEIGHT + (0.5 * NEG_WEIGHT) * curve).astype(BF16).astype(F32)
         grad = tiled * negative - counted * (0.5 - 0.5 * curve)
@@ -315,7 +317,7 @@
             whole(NCOL, 2, CR // NCOL, D),
             half,
             half,
-            whole(64, 128),
+            pl.BlockSpec((64, 128), lambda i: (SLOTS // 64, 0)),
             half,
         ],
         out_specs=[
@@ -333,7 +335,7 @@
             pltpu.VMEM((2, CR, D), F32),
             pltpu.VMEM((HOT, D), F32),
         ],
-        compiler_params=params(56),
+        compiler_params=params(50),
         cost_estimate=cost(28 << 30, 12 << 20),
         name="gradients",
     )(
@@ -466,7 +468,8 @@
     low = first_counts(src_code, ctx_rows)
     low, pieces = lax.optimization_barrier((low, pieces))
     ctx = all_to_all(pick_pieces(matching, pieces), "col")
-    counts = (low, *second_counts(neg_tiles, src_code, ctx_rows))
+    high, second = second_counts(neg_tiles, src_code, ctx_rows)
+    counts = (low, high, high, second)
 
     cold, keep, send = gradients(
         neg_tiles, cold_count, src_code, ctx_rows, vertex_panel, hot_table, hot_map[0],

time: 145 us -> 143 us (0.986)
  Pallas kernels: 62.2 us -> 60 us
    pallas_call x1, Pallas kernels: 24.7 us -> 22.5 us  [gradients(): pl.pallas_call(main_kernel, out_shape=[jax.ShapeDtypeStruct((NCOL, CAP, D...]
where the time goes in v3:
time: 143 us; the launch traced here: 142 us
  Pallas kernels  60 us (42%)
  blocking collectives  32.7 us (23%)
  starting transfers between devices  31.7 us (22%)
  waiting for transfers between devices  13.9 us (10%)
  other arithmetic  2 us (1%)
    all_to_all x2, blocking collectives, all_to_all(): return lax.all_to_all(x, axes, 0, 0, tiled=True)  32.7 us
    pallas_call x1, Pallas kernels, gradients(): pl.pallas_call(main_kernel, out_shape=[jax.ShapeDtypeStruct((NCOL, CAP, D...  22.5 us
    all_to_all x3, starting transfers between devices, all_to_all(): return lax.all_to_all(x, axes, 0, 0, tiled=True)  21.9 us
    pallas_call x1, Pallas kernels, second_counts(): pl.pallas_call(second_count_kernel, out_shape=[jax.ShapeDtypeStruct(shape...  19.4 us
    ppermute x3, waiting for transfers between devices, body(): lax.ppermute(parts[k].astype(BF16), 'x', [(i, i ^ k) for i in range(NX)])  13.6 us
    pallas_call x1, Pallas kernels, first_counts(): pl.pallas_call(first_count_kernel, out_shape=jax.ShapeDtypeStruct((SLOTS,...  10.2 us
    ppermute x1, starting transfers between devices, body(): other = lax.ppermute(own, 'core', swap)  4.25 us
    ppermute x3, starting transfers between devices, body(): lax.ppermute(parts[k].astype(BF16), 'x', [(i, i ^ k) for i in range(NX)])  3.94 us
  transfers between devices with their start and end apart: 8, of which 4 were waited for; matrix products, arithmetic and copies ran while one was open for 1% of the time, Pallas kernels for 23%

profile of v3, /device:TPU:1, one launch (start us, length us, event | category | flops | bytes accessed | tf_op | source)
XLA Modules:
  0.0 142.2 jit_solution(3241213642918753859)
XLA Ops:
  0.6 8.6 %all-to-all-start = ((bf16[16,32,512]{2,1,0:T(8,128)(2,1)}), bf16[16,32,512]{2,1,0:T(8,128)(2,1)S(1)}, u32[]{:S(2)}, u32[]{:S(2)}) async-start(bf16[16,32,512]{2,1,0:T(8,128)(2,1)} %bitcast.16), calls=%async_computation | async-start | bytes 1048576 | tf_op jit(solution)/shard_map/all_to_all | solution.py:449
  9.2 0.0 copy-start.4
  9.3 10.2 %first_counts.1.pairs0_low = f32[1280,256]{1,0:T(8,128)} custom-call(s32[1,1,2,128,128]{4,3,2,1,0:T(8,128)} %codes.3, s32[1,1,2,128,128]{4,3,2,1,0:T(8,128)} %rows.3), custom_call_target="tpu_custom_call" | custom-call | flops 5368709120 | bytes 3145728 | tf_op jit(solution)/shard_map/first_counts/pallas_call | solution.py:139
  19.4 0.3 all-to-all-done.pieces
  19.8 1.6 %pick_pieces.1 = bf16[16,2,32,512]{3,2,1,0:T(8,128)(2,1)} custom-call(s32[2,16]{1,0:T(2,128)S(1)} %copy-done.4, bf16[16,32,512]{2,1,0:T(8,128)(2,1)S(1)} %all-to-all-done.pieces), custom_call_target="tpu_custom_call" | custom-call | bytes 2097152 | tf_op jit(solution)/shard_map/pick_pieces/pallas_call | solution.py:181
  21.4 6.3 %all-to-all-start.1 = ((bf16[16,2,32,512]{3,2,1,0:T(8,128)(2,1)}), bf16[16,2,32,512]{3,2,1,0:T(8,128)(2,1)S(1)}, u32[]{:S(2)}, u32[]{:S(2)}) async-start(bf16[16,2,32,512]{3,2,1,0:T(8,128)(2,1)} %pick_pieces.1), calls=%async_computation.1 | async-start | bytes 2097152 | tf_op jit(solution)/shard_map/all_to_all | solution.py:449
  27.7 0.0 copy-start.1
  27.7 0.0 copy-start.2
  27.7 0.0 copy-start.3
  27.7 0.0 copy-start.7
  27.8 0.0 copy-start.8
  27.8 19.4 %second_counts.1 = (f32[1344,256]{1,0:T(8,128)}, f32[1280,256]{1,0:T(8,128)}) custom-call(s32[1,1,2,128]{3,2,1,0:T(2,128)} %tiles.3, s32[1,1,2,128,128]{4,3,2,1,0:T(8,128)} %codes.3, s32[1,1,2,128,128]{4,3,2,1,0:T(8,128)} %rows.3, s32[1,1,2,128,128]{4,3,2,1,0:T(8,128)} %codes.3, s32[1,1,2,128,128]{4,3,2,1,0:T(8,128)} %rows.3), custom_call_target="tpu_custom_call" | custom-call | flops 10737418240 | bytes 6291456 | tf_op jit(solution)/shard_map/second_counts/pallas_call | solution.py:154
  47.2 0.0 copy-start.9
  47.2 1.0 copy-done.9
  48.2 22.5 %gradients.1 = (bf16[16,64,512]{2,1,0:T(8,128)(2,1)}, f32[4,256,512]{2,1,0:T(8,128)}, bf16[4,256,512]{2,1,0:T(8,128)(2,1)S(1)}) custom-call(s32[1,1,2,128]{3,2,1,0:T(2,128)S(1)} %copy-done.7, s32[1,16,16]{2,1,0:T(8,128)S(1)} %copy-done.3, s32[1,1,2,128,128]{4,3,2,1,0:T(8,128)S(1)} %copy-done.5, s32[1,1,2,128,128]{4,3,2,1,0:T(8,128)S(1)} %copy-done.6, ...), custom_call_target="tpu_custom_call" | custom-call | flops 30064771072 | bytes 12582912 | tf_op jit(solution)/shard_map/gradients/pallas_call | solution.py:304
  70.7 1.6 %collective-permute-start = (bf16[4,256,512]{2,1,0:T(8,128)(2,1)S(1)}, bf16[4,256,512]{2,1,0:T(8,128)(2,1)S(1)}, u32[]{:S(2)}, u32[]{:S(2)}) collective-permute-start(bf16[4,256,512]{2,1,0:T(8,128)(2,1)S(1)} %get-tuple-element.20), channel_id=1, source_target_pairs={{0,16},{16,0},{1,17},{17,1},{2,18},{18,2},{3,19},{19,3},{4,20},{20... | collective-permute-start | bytes 3145736 | tf_op jit(solution)/shard_map/ppermute | solution.py:479
  72.3 7.0 %all-to-all-start.2 = ((bf16[16,64,512]{2,1,0:T(8,128)(2,1)}), bf16[16,64,512]{2,1,0:T(8,128)(2,1)}, u32[]{:S(2)}, u32[]{:S(2)}) async-start(bf16[16,64,512]{2,1,0:T(8,128)(2,1)} %get-tuple-element.18), calls=%async_computation.2 | async-start | bytes 2097152 | tf_op jit(solution)/shard_map/all_to_all | solution.py:449
  79.3 2.0 %fusion = (bf16[4,256,512]{2,1,0:T(8,128)(2,1)S(1)}, f32[4,256,512]{2,1,0:T(8,128)S(1)}) fusion(f32[4,256,512]{2,1,0:T(8,128)} %get-tuple-element.19, bf16[4,256,512]{2,1,0:T(8,128)(2,1)S(1)} %collective-permute-done), kind=kLoop, calls=%fused_computation.5 | loop fusion | flops 1572864 | bytes 6291456 | tf_op jit(solution)/shard_map/convert.2
  81.3 0.1 slice_bitcast_fusion.1
  81.4 1.3 collective-permute-start.1
  82.7 2.5 %collective-permute-start.2 = (bf16[256,512]{1,0:T(8,128)(2,1)S(1)}, bf16[256,512]{1,0:T(8,128)(2,1)S(1)}, u32[]{:S(2)}, u32[]{:S(2)}) collective-permute-start(bf16[256,512]{1,0:T(8,128)(2,1)S(1)} %get-tuple-element.28), channel_id=1, source_target_pairs={{0,64},{32,96},{64,0},{96,32},{1,65},{33,97},{65,1},{97,33},{2,66}... | collective-permute-start | bytes 786440 | tf_op jit(solution)/shard_map/ppermute | solution.py:482
  85.1 0.2 collective-permute-start.3
  85.4 3.7 %collective-permute-done.1.first = bf16[256,512]{1,0:T(8,128)(2,1)S(1)} collective-permute-done((bf16[256,512]{1,0:T(8,128)(2,1)S(1)}, bf16[256,512]{1,0:T(8,128)(2,1)S(1)}, u32[]{:S(2)}, u32[]{:S(2)}) %collective-permute-start.1) | collective-permute-done | bytes 262176 | tf_op jit(solution)/shard_map/ppermute | solution.py:482
  89.1 8.0 %collective-permute-done.2.second = bf16[256,512]{1,0:T(8,128)(2,1)S(1)} collective-permute-done((bf16[256,512]{1,0:T(8,128)(2,1)S(1)}, bf16[256,512]{1,0:T(8,128)(2,1)S(1)}, u32[]{:S(2)}, u32[]{:S(2)}) %collective-permute-start.2) | collective-permute-done | bytes 262176 | tf_op jit(solution)/shard_map/ppermute | solution.py:482
  97.0 1.9 %collective-permute-done.3.third = bf16[256,512]{1,0:T(8,128)(2,1)S(1)} collective-permute-done((bf16[256,512]{1,0:T(8,128)(2,1)S(1)}, bf16[256,512]{1,0:T(8,128)(2,1)S(1)}, u32[]{:S(2)}, u32[]{:S(2)}) %collective-permute-start.3) | collective-permute-done | bytes 262176 | tf_op jit(solution)/shard_map/ppermute | solution.py:482
  98.9 0.1 x_sum.1
  99.1 13.6 %all_to_all.25.parts = bf16[16,16,512]{2,1,0:T(8,128)(2,1)S(1)} all-to-all(bf16[16,16,512]{2,1,0:T(8,128)(2,1)S(1)} %x_sum.1), channel_id=1, replica_groups=mesh['x'=4,'core'=2,'col'=16] {'col'}, dimensions={0} | all-to-all | bytes 524288 | tf_op jit(solution)/shard_map/all_to_all | solution.py:449
  112.7 0.7 col_sum.1
  113.4 19.1 %all_to_all.26 = bf16[64,16,512]{2,1,0:T(8,128)(2,1)S(1)} all-to-all(bf16[64,16,512]{2,1,0:T(8,128)(2,1)S(1)} %bitcast.15), channel_id=1, replica_groups=mesh['x'=4,'core'=2,'col'=16] {'x','col'}, dimensions={0} | all-to-all | bytes 2097152 | tf_op jit(solution)/shard_map/all_to_all | solution.py:449
  132.4 4.2 %collective-permute-start.4 = (bf16[4,16,16,512]{3,2,1,0:T(8,128)(2,1)S(1)}, bf16[4,16,16,512]{3,2,1,0:T(8,128)(2,1)S(1)}, u32[]{:S(2)}, u32[]{:S(2)}) collective-permute-start(bf16[4,16,16,512]{3,2,1,0:T(8,128)(2,1)S(1)} %bitcast.13), channel_id=1, source_target_pairs={{0,16},{16,0},{1,17},{17,1},{2,18},{18,2},{3,19},{19,3},{4,20},{20... | collective-permute-start | bytes 3145736 | tf_op jit(solution)/shard_map/ppermute | solution.py:490
  136.7 3.4 %vertex_rows.1 = f32[256,512]{1,0:T(8,128)} custom-call(s32[1]{0:T(128)} %bitcast.col, s32[1,16,16]{2,1,0:T(8,128)} %cold_count.3, s32[1,16,16,64]{3,2,1,0:T(8,128)} %cold_list.3, bf16[16,64,512]{2,1,0:T(8,128)(2,1)} %all-to-all-done.2.received, bf16[4096,512]{1,0:T(8,128)(2,1)} %panel.3), custom_call_target="tpu_custom_call" | custom-call | flops 268435456 | bytes 2097152 | tf_op jit(solution)/shard_map/vertex_rows/pallas_call | solution.py:428
  140.1 2.1 %finish.1 = (f32[1024,512]{1,0:T(8,128)}, f32[512,512]{1,0:T(8,128)}) custom-call(bf16[4,16,16,512]{3,2,1,0:T(8,128)(2,1)S(1)} %bitcast.14, bf16[4,16,16,512]{3,2,1,0:T(8,128)(2,1)S(1)} %collective-permute-done.4.other, bf16[1024,512]{1,0:T(8,128)(2,1)S(1)} %copy-done.1, bf16[512,512]{1,0:T(8,128)(2,1)S(1)} %copy-done), custom_call_target="tpu_custom_call" | custom-call | flops 1048576 | bytes 7340032 | tf_op jit(solution)/shard_map/finish/pallas_call | solution.py:407
  (17 shorter events, 0.1 us)
Async XLA Ops:
  0.6 19.1 %all-to-all-start = ((bf16[16,32,512]{2,1,0:T(8,128)(2,1)}), bf16[16,32,512]{2,1,0:T(8,128)(2,1)S(1)}, u32[]{:S(2)}, u32[]{:S(2)}) async-start(bf16[16,32,512]{2,1,0:T(8,128)(2,1)} %bitcast.16), calls=%async_computation | async-start | bytes 1048576 | tf_op jit(solution)/shard_map/all_to_all | solution.py:449
  9.2 10.5 %copy-start.4 = (s32[2,16]{1,0:T(2,128)S(1)}, s32[2,16]{1,0:T(2,128)}, u32[]{:S(2)}) copy-start(s32[2,16]{1,0:T(2,128)} %matching.3) | copy-start | bytes 388
  21.4 25.8 %all-to-all-start.1 = ((bf16[16,2,32,512]{3,2,1,0:T(8,128)(2,1)}), bf16[16,2,32,512]{3,2,1,0:T(8,128)(2,1)S(1)}, u32[]{:S(2)}, u32[]{:S(2)}) async-start(bf16[16,2,32,512]{3,2,1,0:T(8,128)(2,1)} %pick_pieces.1), calls=%async_computation.1 | async-start | bytes 2097152 | tf_op jit(solution)/shard_map/all_to_all | solution.py:449
  27.7 20.5 %copy-start.1 = (bf16[1024,512]{1,0:T(8,128)(2,1)S(1)}, bf16[1024,512]{1,0:T(8,128)(2,1)}, u32[]{:S(2)}) copy-start(bf16[1024,512]{1,0:T(8,128)(2,1)} %hot_table.3) | copy-start | bytes 3145732
  27.7 20.5 %copy-start.2 = (s32[1,16,16,64]{3,2,1,0:T(8,128)S(1)}, s32[1,16,16,64]{3,2,1,0:T(8,128)}, u32[]{:S(2)}) copy-start(s32[1,16,16,64]{3,2,1,0:T(8,128)} %cold_list.3) | copy-start | bytes 196612
  27.7 20.5 %copy-start.3 = (s32[1,16,16]{2,1,0:T(8,128)S(1)}, s32[1,16,16]{2,1,0:T(8,128)}, u32[]{:S(2)}) copy-start(s32[1,16,16]{2,1,0:T(8,128)} %cold_count.3) | copy-start | bytes 3076
  27.7 20.4 %copy-start.5 = (s32[1,1,2,128,128]{4,3,2,1,0:T(8,128)S(1)}, s32[1,1,2,128,128]{4,3,2,1,0:T(8,128)}, u32[]{:S(2)}) copy-start(s32[1,1,2,128,128]{4,3,2,1,0:T(8,128)} %codes.3) | copy-start | bytes 393220
  27.7 20.4 %copy-start.6 = (s32[1,1,2,128,128]{4,3,2,1,0:T(8,128)S(1)}, s32[1,1,2,128,128]{4,3,2,1,0:T(8,128)}, u32[]{:S(2)}) copy-start(s32[1,1,2,128,128]{4,3,2,1,0:T(8,128)} %rows.3) | copy-start | bytes 393220
  27.7 20.4 %copy-start.7 = (s32[1,1,2,128]{3,2,1,0:T(2,128)S(1)}, s32[1,1,2,128]{3,2,1,0:T(2,128)}, u32[]{:S(2)}) copy-start(s32[1,1,2,128]{3,2,1,0:T(2,128)} %tiles.3) | copy-start | bytes 3076
  27.8 20.4 %copy-start.8 = (s32[1,1,256]{2,1,0:T(1,128)S(1)}, s32[1,1,256]{2,1,0:T(1,128)}, u32[]{:S(2)}) copy-start(s32[1,1,256]{2,1,0:T(1,128)} %param.14) | copy-start | bytes 3076
  47.2 1.0 copy-start.9
  70.7 8.6 %collective-permute-start = (bf16[4,256,512]{2,1,0:T(8,128)(2,1)S(1)}, bf16[4,256,512]{2,1,0:T(8,128)(2,1)S(1)}, u32[]{:S(2)}, u32[]{:S(2)}) collective-permute-start(bf16[4,256,512]{2,1,0:T(8,128)(2,1)S(1)} %get-tuple-element.20), channel_id=1, source_target_pairs={{0,16},{16,0},{1,17},{17,1},{2,18},{18,2},{3,19},{19,3},{4,20},{20... | collective-permute-start | bytes 3145736 | tf_op jit(solution)/shard_map/ppermute | solution.py:479
  72.3 26.7 %all-to-all-start.2 = ((bf16[16,64,512]{2,1,0:T(8,128)(2,1)}), bf16[16,64,512]{2,1,0:T(8,128)(2,1)}, u32[]{:S(2)}, u32[]{:S(2)}) async-start(bf16[16,64,512]{2,1,0:T(8,128)(2,1)} %get-tuple-element.18), calls=%async_computation.2 | async-start | bytes 2097152 | tf_op jit(solution)/shard_map/all_to_all | solution.py:449
  81.4 7.7 %collective-permute-start.1 = (bf16[256,512]{1,0:T(8,128)(2,1)S(1)}, bf16[256,512]{1,0:T(8,128)(2,1)S(1)}, u32[]{:S(2)}, u32[]{:S(2)}) collective-permute-start(bf16[256,512]{1,0:T(8,128)(2,1)S(1)} %get-tuple-element.29), channel_id=1, source_target_pairs={{0,32},{32,0},{64,96},{96,64},{1,33},{33,1},{65,97},{97,65},{2,34}... | collective-permute-start | bytes 786440 | tf_op jit(solution)/shard_map/ppermute | solution.py:482
  82.7 14.4 %collective-permute-start.2 = (bf16[256,512]{1,0:T(8,128)(2,1)S(1)}, bf16[256,512]{1,0:T(8,128)(2,1)S(1)}, u32[]{:S(2)}, u32[]{:S(2)}) collective-permute-start(bf16[256,512]{1,0:T(8,128)(2,1)S(1)} %get-tuple-element.28), channel_id=1, source_target_pairs={{0,64},{32,96},{64,0},{96,32},{1,65},{33,97},{65,1},{97,33},{2,66}... | collective-permute-start | bytes 786440 | tf_op jit(solution)/shard_map/ppermute | solution.py:482
  85.1 13.8 %collective-permute-start.3 = (bf16[256,512]{1,0:T(8,128)(2,1)S(1)}, bf16[256,512]{1,0:T(8,128)(2,1)S(1)}, u32[]{:S(2)}, u32[]{:S(2)}) collective-permute-start(bf16[256,512]{1,0:T(8,128)(2,1)S(1)} %get-tuple-element.27), channel_id=1, source_target_pairs={{0,96},{32,64},{64,32},{96,0},{1,97},{33,65},{65,33},{97,1},{2,98}... | collective-permute-start | bytes 786440 | tf_op jit(solution)/shard_map/ppermute | solution.py:482
  132.4 7.6 %collective-permute-start.4 = (bf16[4,16,16,512]{3,2,1,0:T(8,128)(2,1)S(1)}, bf16[4,16,16,512]{3,2,1,0:T(8,128)(2,1)S(1)}, u32[]{:S(2)}, u32[]{:S(2)}) collective-permute-start(bf16[4,16,16,512]{3,2,1,0:T(8,128)(2,1)S(1)} %bitcast.13), channel_id=1, source_target_pairs={{0,16},{16,0},{1,17},{17,1},{2,18},{18,2},{3,19},{19,3},{4,20},{20... | collective-permute-start | bytes 3145736 | tf_op jit(solution)/shard_map/ppermute | solution.py:490
  136.7 3.4 %copy-start = (bf16[512,512]{1,0:T(8,128)(2,1)S(1)}, bf16[512,512]{1,0:T(8,128)(2,1)}, u32[]{:S(2)}) copy-start(bf16[512,512]{1,0:T(8,128)(2,1)} %context.1) | copy-start | bytes 1572868

commit v4 on v3

--- a/solution.py
+++ b/solution.py
@@ -335,7 +335,7 @@
             pltpu.VMEM((2, CR, D), F32),
             pltpu.VMEM((HOT, D), F32),
         ],
-        compiler_params=params(50),
+        compiler_params=params(49),
         cost_estimate=cost(28 << 30, 12 << 20),
         name="gradients",
     )(

time: 143 us -> 142 us (level)
  no operation moved by 1% of the time
where the time goes in v4:
time: 142 us; the launch traced here: 141 us
  Pallas kernels  60.1 us (42%)
  blocking collectives  32.8 us (23%)
  starting transfers between devices  31.7 us (22%)
  waiting for transfers between devices  13.9 us (10%)
  other arithmetic  2 us (1%)
    all_to_all x2, blocking collectives, all_to_all(): return lax.all_to_all(x, axes, 0, 0, tiled=True)  32.8 us
    pallas_call x1, Pallas kernels, gradients(): pl.pallas_call(main_kernel, out_shape=[jax.ShapeDtypeStruct((NCOL, CAP, D...  22.7 us
    all_to_all x3, starting transfers between devices, all_to_all(): return lax.all_to_all(x, axes, 0, 0, tiled=True)  21.9 us
    pallas_call x1, Pallas kernels, second_counts(): pl.pallas_call(second_count_kernel, out_shape=[jax.ShapeDtypeStruct(shape...  19.4 us
    ppermute x3, waiting for transfers between devices, body(): lax.ppermute(parts[k].astype(BF16), 'x', [(i, i ^ k) for i in range(NX)])  13.5 us
    pallas_call x1, Pallas kernels, first_counts(): pl.pallas_call(first_count_kernel, out_shape=jax.ShapeDtypeStruct((SLOTS,...  10.2 us
    ppermute x1, starting transfers between devices, body(): other = lax.ppermute(own, 'core', swap)  4.25 us
    ppermute x3, starting transfers between devices, body(): lax.ppermute(parts[k].astype(BF16), 'x', [(i, i ^ k) for i in range(NX)])  3.94 us
  transfers between devices with their start and end apart: 8, of which 4 were waited for; matrix products, arithmetic and copies ran while one was open for 1% of the time, Pallas kernels for 23%

profile of v4, /device:TPU:1, one launch (start us, length us, event | category | flops | bytes accessed | tf_op | source)
XLA Modules:
  0.0 141.4 jit_solution(18426463858748447593)
XLA Ops:
  0.6 8.6 %all-to-all-start = ((bf16[16,32,512]{2,1,0:T(8,128)(2,1)}), bf16[16,32,512]{2,1,0:T(8,128)(2,1)S(1)}, u32[]{:S(2)}, u32[]{:S(2)}) async-start(bf16[16,32,512]{2,1,0:T(8,128)(2,1)} %bitcast.16), calls=%async_computation | async-start | bytes 1048576 | tf_op jit(solution)/shard_map/all_to_all | solution.py:449
  9.2 0.0 copy-start.4
  9.3 10.2 %first_counts.1.pairs0_low = f32[1280,256]{1,0:T(8,128)} custom-call(s32[1,1,2,128,128]{4,3,2,1,0:T(8,128)} %codes.3, s32[1,1,2,128,128]{4,3,2,1,0:T(8,128)} %rows.3), custom_call_target="tpu_custom_call" | custom-call | flops 5368709120 | bytes 3145728 | tf_op jit(solution)/shard_map/first_counts/pallas_call | solution.py:139
  19.4 0.3 all-to-all-done.pieces
  19.8 1.6 %pick_pieces.1 = bf16[16,2,32,512]{3,2,1,0:T(8,128)(2,1)} custom-call(s32[2,16]{1,0:T(2,128)S(1)} %copy-done.4, bf16[16,32,512]{2,1,0:T(8,128)(2,1)S(1)} %all-to-all-done.pieces), custom_call_target="tpu_custom_call" | custom-call | bytes 2097152 | tf_op jit(solution)/shard_map/pick_pieces/pallas_call | solution.py:181
  21.4 6.3 %all-to-all-start.1 = ((bf16[16,2,32,512]{3,2,1,0:T(8,128)(2,1)}), bf16[16,2,32,512]{3,2,1,0:T(8,128)(2,1)S(1)}, u32[]{:S(2)}, u32[]{:S(2)}) async-start(bf16[16,2,32,512]{3,2,1,0:T(8,128)(2,1)} %pick_pieces.1), calls=%async_computation.1 | async-start | bytes 2097152 | tf_op jit(solution)/shard_map/all_to_all | solution.py:449
  27.7 0.0 copy-start.1
  27.7 0.0 copy-start.2
  27.7 0.0 copy-start.3
  27.7 0.0 copy-start.5
  27.7 0.0 copy-start.7
  27.8 0.0 copy-start.8
  27.8 19.4 %second_counts.1 = (f32[1344,256]{1,0:T(8,128)}, f32[1280,256]{1,0:T(8,128)}) custom-call(s32[1,1,2,128]{3,2,1,0:T(2,128)} %tiles.3, s32[1,1,2,128,128]{4,3,2,1,0:T(8,128)} %codes.3, s32[1,1,2,128,128]{4,3,2,1,0:T(8,128)} %rows.3, s32[1,1,2,128,128]{4,3,2,1,0:T(8,128)} %codes.3, s32[1,1,2,128,128]{4,3,2,1,0:T(8,128)} %rows.3), custom_call_target="tpu_custom_call" | custom-call | flops 10737418240 | bytes 6291456 | tf_op jit(solution)/shard_map/second_counts/pallas_call | solution.py:154
  47.3 22.7 %gradients.1 = (bf16[16,64,512]{2,1,0:T(8,128)(2,1)}, f32[4,256,512]{2,1,0:T(8,128)}, bf16[4,256,512]{2,1,0:T(8,128)(2,1)}) custom-call(s32[1,1,2,128]{3,2,1,0:T(2,128)S(1)} %copy-done.7, s32[1,16,16]{2,1,0:T(8,128)S(1)} %copy-done.3, s32[1,1,2,128,128]{4,3,2,1,0:T(8,128)S(1)} %copy-done.5, s32[1,1,2,128,128]{4,3,2,1,0:T(8,128)S(1)} %copy-done.6, ...), custom_call_target="tpu_custom_call" | custom-call | flops 30064771072 | bytes 12582912 | tf_op jit(solution)/shard_map/gradients/pallas_call | solution.py:304
  69.9 1.6 %collective-permute-start = (bf16[4,256,512]{2,1,0:T(8,128)(2,1)}, bf16[4,256,512]{2,1,0:T(8,128)(2,1)S(1)}, u32[]{:S(2)}, u32[]{:S(2)}) collective-permute-start(bf16[4,256,512]{2,1,0:T(8,128)(2,1)} %get-tuple-element.20), channel_id=1, source_target_pairs={{0,16},{16,0},{1,17},{17,1},{2,18},{18,2},{3,19},{19,3},{4,20},{20... | collective-permute-start | bytes 3145736 | tf_op jit(solution)/shard_map/ppermute | solution.py:479
  71.5 6.9 %all-to-all-start.2 = ((bf16[16,64,512]{2,1,0:T(8,128)(2,1)}), bf16[16,64,512]{2,1,0:T(8,128)(2,1)S(1)}, u32[]{:S(2)}, u32[]{:S(2)}) async-start(bf16[16,64,512]{2,1,0:T(8,128)(2,1)} %get-tuple-element.18), calls=%async_computation.2 | async-start | bytes 2097152 | tf_op jit(solution)/shard_map/all_to_all | solution.py:449
  78.5 2.0 %fusion = (bf16[4,256,512]{2,1,0:T(8,128)(2,1)S(1)}, f32[4,256,512]{2,1,0:T(8,128)S(1)}) fusion(f32[4,256,512]{2,1,0:T(8,128)} %get-tuple-element.19, bf16[4,256,512]{2,1,0:T(8,128)(2,1)S(1)} %collective-permute-done), kind=kLoop, calls=%fused_computation.5 | loop fusion | flops 1572864 | bytes 6291456 | tf_op jit(solution)/shard_map/convert.2
  80.5 0.1 slice_bitcast_fusion.1
  80.6 1.3 collective-permute-start.1
  81.9 2.4 %collective-permute-start.2 = (bf16[256,512]{1,0:T(8,128)(2,1)S(1)}, bf16[256,512]{1,0:T(8,128)(2,1)S(1)}, u32[]{:S(2)}, u32[]{:S(2)}) collective-permute-start(bf16[256,512]{1,0:T(8,128)(2,1)S(1)} %get-tuple-element.28), channel_id=1, source_target_pairs={{0,64},{32,96},{64,0},{96,32},{1,65},{33,97},{65,1},{97,33},{2,66}... | collective-permute-start | bytes 786440 | tf_op jit(solution)/shard_map/ppermute | solution.py:482
  84.3 0.2 collective-permute-start.3
  84.5 3.7 %collective-permute-done.1.first = bf16[256,512]{1,0:T(8,128)(2,1)S(1)} collective-permute-done((bf16[256,512]{1,0:T(8,128)(2,1)S(1)}, bf16[256,512]{1,0:T(8,128)(2,1)S(1)}, u32[]{:S(2)}, u32[]{:S(2)}) %collective-permute-start.1) | collective-permute-done | bytes 262176 | tf_op jit(solution)/shard_map/ppermute | solution.py:482
  88.2 7.9 %collective-permute-done.2.second = bf16[256,512]{1,0:T(8,128)(2,1)S(1)} collective-permute-done((bf16[256,512]{1,0:T(8,128)(2,1)S(1)}, bf16[256,512]{1,0:T(8,128)(2,1)S(1)}, u32[]{:S(2)}, u32[]{:S(2)}) %collective-permute-start.2) | collective-permute-done | bytes 262176 | tf_op jit(solution)/shard_map/ppermute | solution.py:482
  96.1 2.0 %collective-permute-done.3.third = bf16[256,512]{1,0:T(8,128)(2,1)S(1)} collective-permute-done((bf16[256,512]{1,0:T(8,128)(2,1)S(1)}, bf16[256,512]{1,0:T(8,128)(2,1)S(1)}, u32[]{:S(2)}, u32[]{:S(2)}) %collective-permute-start.3) | collective-permute-done | bytes 262176 | tf_op jit(solution)/shard_map/ppermute | solution.py:482
  98.1 0.1 x_sum.1
  98.2 0.0 copy-start.9
  98.2 13.7 %all_to_all.25.parts = bf16[16,16,512]{2,1,0:T(8,128)(2,1)S(1)} all-to-all(bf16[16,16,512]{2,1,0:T(8,128)(2,1)S(1)} %x_sum.1), channel_id=1, replica_groups=mesh['x'=4,'core'=2,'col'=16] {'col'}, dimensions={0} | all-to-all | bytes 524288 | tf_op jit(solution)/shard_map/all_to_all | solution.py:449
  111.9 0.7 col_sum.1
  112.6 19.1 %all_to_all.26 = bf16[64,16,512]{2,1,0:T(8,128)(2,1)S(1)} all-to-all(bf16[64,16,512]{2,1,0:T(8,128)(2,1)S(1)} %bitcast.15), channel_id=1, replica_groups=mesh['x'=4,'core'=2,'col'=16] {'x','col'}, dimensions={0} | all-to-all | bytes 2097152 | tf_op jit(solution)/shard_map/all_to_all | solution.py:449
  131.7 4.2 %collective-permute-start.4 = (bf16[4,16,16,512]{3,2,1,0:T(8,128)(2,1)S(1)}, bf16[4,16,16,512]{3,2,1,0:T(8,128)(2,1)S(1)}, u32[]{:S(2)}, u32[]{:S(2)}) collective-permute-start(bf16[4,16,16,512]{3,2,1,0:T(8,128)(2,1)S(1)} %bitcast.13), channel_id=1, source_target_pairs={{0,16},{16,0},{1,17},{17,1},{2,18},{18,2},{3,19},{19,3},{4,20},{20... | collective-permute-start | bytes 3145736 | tf_op jit(solution)/shard_map/ppermute | solution.py:490
  135.9 3.4 %vertex_rows.1 = f32[256,512]{1,0:T(8,128)} custom-call(s32[1]{0:T(128)} %bitcast.col, s32[1,16,16]{2,1,0:T(8,128)} %cold_count.3, s32[1,16,16,64]{3,2,1,0:T(8,128)} %cold_list.3, bf16[16,64,512]{2,1,0:T(8,128)(2,1)} %copy-done.9, bf16[4096,512]{1,0:T(8,128)(2,1)} %panel.3), custom_call_target="tpu_custom_call" | custom-call | flops 268435456 | bytes 2097152 | tf_op jit(solution)/shard_map/vertex_rows/pallas_call | solution.py:428
  139.3 2.1 %finish.1 = (f32[1024,512]{1,0:T(8,128)}, f32[512,512]{1,0:T(8,128)}) custom-call(bf16[4,16,16,512]{3,2,1,0:T(8,128)(2,1)S(1)} %bitcast.14, bf16[4,16,16,512]{3,2,1,0:T(8,128)(2,1)S(1)} %collective-permute-done.4.other, bf16[1024,512]{1,0:T(8,128)(2,1)S(1)} %copy-done.1, bf16[512,512]{1,0:T(8,128)(2,1)S(1)} %copy-done), custom_call_target="tpu_custom_call" | custom-call | flops 1048576 | bytes 7340032 | tf_op jit(solution)/shard_map/finish/pallas_call | solution.py:407
  (17 shorter events, 0.1 us)
Async XLA Ops:
  0.6 19.1 %all-to-all-start = ((bf16[16,32,512]{2,1,0:T(8,128)(2,1)}), bf16[16,32,512]{2,1,0:T(8,128)(2,1)S(1)}, u32[]{:S(2)}, u32[]{:S(2)}) async-start(bf16[16,32,512]{2,1,0:T(8,128)(2,1)} %bitcast.16), calls=%async_computation | async-start | bytes 1048576 | tf_op jit(solution)/shard_map/all_to_all | solution.py:449
  9.2 10.5 %copy-start.4 = (s32[2,16]{1,0:T(2,128)S(1)}, s32[2,16]{1,0:T(2,128)}, u32[]{:S(2)}) copy-start(s32[2,16]{1,0:T(2,128)} %matching.3) | copy-start | bytes 388
  21.4 25.8 %all-to-all-start.1 = ((bf16[16,2,32,512]{3,2,1,0:T(8,128)(2,1)}), bf16[16,2,32,512]{3,2,1,0:T(8,128)(2,1)S(1)}, u32[]{:S(2)}, u32[]{:S(2)}) async-start(bf16[16,2,32,512]{3,2,1,0:T(8,128)(2,1)} %pick_pieces.1), calls=%async_computation.1 | async-start | bytes 2097152 | tf_op jit(solution)/shard_map/all_to_all | solution.py:449
  27.7 19.5 %copy-start.1 = (bf16[1024,512]{1,0:T(8,128)(2,1)S(1)}, bf16[1024,512]{1,0:T(8,128)(2,1)}, u32[]{:S(2)}) copy-start(bf16[1024,512]{1,0:T(8,128)(2,1)} %hot_table.3) | copy-start | bytes 3145732
  27.7 19.5 %copy-start.2 = (s32[1,16,16,64]{3,2,1,0:T(8,128)S(1)}, s32[1,16,16,64]{3,2,1,0:T(8,128)}, u32[]{:S(2)}) copy-start(s32[1,16,16,64]{3,2,1,0:T(8,128)} %cold_list.3) | copy-start | bytes 196612
  27.7 19.5 %copy-start.3 = (s32[1,16,16]{2,1,0:T(8,128)S(1)}, s32[1,16,16]{2,1,0:T(8,128)}, u32[]{:S(2)}) copy-start(s32[1,16,16]{2,1,0:T(8,128)} %cold_count.3) | copy-start | bytes 3076
  27.7 19.5 %copy-start.5 = (s32[1,1,2,128,128]{4,3,2,1,0:T(8,128)S(1)}, s32[1,1,2,128,128]{4,3,2,1,0:T(8,128)}, u32[]{:S(2)}) copy-start(s32[1,1,2,128,128]{4,3,2,1,0:T(8,128)} %codes.3) | copy-start | bytes 393220
  27.7 19.5 %copy-start.6 = (s32[1,1,2,128,128]{4,3,2,1,0:T(8,128)S(1)}, s32[1,1,2,128,128]{4,3,2,1,0:T(8,128)}, u32[]{:S(2)}) copy-start(s32[1,1,2,128,128]{4,3,2,1,0:T(8,128)} %rows.3) | copy-start | bytes 393220
  27.7 19.5 %copy-start.7 = (s32[1,1,2,128]{3,2,1,0:T(2,128)S(1)}, s32[1,1,2,128]{3,2,1,0:T(2,128)}, u32[]{:S(2)}) copy-start(s32[1,1,2,128]{3,2,1,0:T(2,128)} %tiles.3) | copy-start | bytes 3076
  27.8 19.5 %copy-start.8 = (s32[1,1,256]{2,1,0:T(1,128)S(1)}, s32[1,1,256]{2,1,0:T(1,128)}, u32[]{:S(2)}) copy-start(s32[1,1,256]{2,1,0:T(1,128)} %param.14) | copy-start | bytes 3076
  69.9 8.5 %collective-permute-start = (bf16[4,256,512]{2,1,0:T(8,128)(2,1)}, bf16[4,256,512]{2,1,0:T(8,128)(2,1)S(1)}, u32[]{:S(2)}, u32[]{:S(2)}) collective-permute-start(bf16[4,256,512]{2,1,0:T(8,128)(2,1)} %get-tuple-element.20), channel_id=1, source_target_pairs={{0,16},{16,0},{1,17},{17,1},{2,18},{18,2},{3,19},{19,3},{4,20},{20... | collective-permute-start | bytes 3145736 | tf_op jit(solution)/shard_map/ppermute | solution.py:479
  71.5 26.7 %all-to-all-start.2 = ((bf16[16,64,512]{2,1,0:T(8,128)(2,1)}), bf16[16,64,512]{2,1,0:T(8,128)(2,1)S(1)}, u32[]{:S(2)}, u32[]{:S(2)}) async-start(bf16[16,64,512]{2,1,0:T(8,128)(2,1)} %get-tuple-element.18), calls=%async_computation.2 | async-start | bytes 2097152 | tf_op jit(solution)/shard_map/all_to_all | solution.py:449
  80.6 7.7 %collective-permute-start.1 = (bf16[256,512]{1,0:T(8,128)(2,1)S(1)}, bf16[256,512]{1,0:T(8,128)(2,1)S(1)}, u32[]{:S(2)}, u32[]{:S(2)}) collective-permute-start(bf16[256,512]{1,0:T(8,128)(2,1)S(1)} %get-tuple-element.29), channel_id=1, source_target_pairs={{0,32},{32,0},{64,96},{96,64},{1,33},{33,1},{65,97},{97,65},{2,34}... | collective-permute-start | bytes 786440 | tf_op jit(solution)/shard_map/ppermute | solution.py:482
  81.9 14.2 %collective-permute-start.2 = (bf16[256,512]{1,0:T(8,128)(2,1)S(1)}, bf16[256,512]{1,0:T(8,128)(2,1)S(1)}, u32[]{:S(2)}, u32[]{:S(2)}) collective-permute-start(bf16[256,512]{1,0:T(8,128)(2,1)S(1)} %get-tuple-element.28), channel_id=1, source_target_pairs={{0,64},{32,96},{64,0},{96,32},{1,65},{33,97},{65,1},{97,33},{2,66}... | collective-permute-start | bytes 786440 | tf_op jit(solution)/shard_map/ppermute | solution.py:482
  84.3 13.8 %collective-permute-start.3 = (bf16[256,512]{1,0:T(8,128)(2,1)S(1)}, bf16[256,512]{1,0:T(8,128)(2,1)S(1)}, u32[]{:S(2)}, u32[]{:S(2)}) collective-permute-start(bf16[256,512]{1,0:T(8,128)(2,1)S(1)} %get-tuple-element.27), channel_id=1, source_target_pairs={{0,96},{32,64},{64,32},{96,0},{1,97},{33,65},{65,33},{97,1},{2,98}... | collective-permute-start | bytes 786440 | tf_op jit(solution)/shard_map/ppermute | solution.py:482
  98.2 33.5 %copy-start.9 = (bf16[16,64,512]{2,1,0:T(8,128)(2,1)}, bf16[16,64,512]{2,1,0:T(8,128)(2,1)S(1)}, u32[]{:S(2)}) copy-start(bf16[16,64,512]{2,1,0:T(8,128)(2,1)S(1)} %all-to-all-done.2.received) | copy-start | bytes 3145732
  131.7 7.6 %collective-permute-start.4 = (bf16[4,16,16,512]{3,2,1,0:T(8,128)(2,1)S(1)}, bf16[4,16,16,512]{3,2,1,0:T(8,128)(2,1)S(1)}, u32[]{:S(2)}, u32[]{:S(2)}) collective-permute-start(bf16[4,16,16,512]{3,2,1,0:T(8,128)(2,1)S(1)} %bitcast.13), channel_id=1, source_target_pairs={{0,16},{16,0},{1,17},{17,1},{2,18},{18,2},{3,19},{19,3},{4,20},{20... | collective-permute-start | bytes 3145736 | tf_op jit(solution)/shard_map/ppermute | solution.py:490
  135.9 3.4 %copy-start = (bf16[512,512]{1,0:T(8,128)(2,1)S(1)}, bf16[512,512]{1,0:T(8,128)(2,1)}, u32[]{:S(2)}) copy-start(bf16[512,512]{1,0:T(8,128)(2,1)} %context.1) | copy-start | bytes 1572868
